TPU v7x, 32 devices: a whole 2x2x4 slice. The times are simulated.
32 devices in a mesh: windows: 2 (over x), tiles: 16 (over z, y, core).
Axes of the slice: x: 2, y: 2, z: 4, core: 2. Of those that a mesh axis runs over, the one named last changes fastest.
Arguments:
- data: bfloat16 [16, 2, 2048, 128], P('windows', None, 'tiles'), parts along dimension 0, may hold values from -6 to 6
- wavelet: float32 [8, 2], replicated, may hold values from -4 to 4
- panel_block: int32 [1], replicated, may hold values from 0 to 15
- tiles: bfloat16 [512, 2, 128, 128], P(('windows', 'tiles')), parts along dimension 0, may hold values from -0.25 to 0.25
- cover_rows: int32 [512], P(('windows', 'tiles')), parts along dimension 0, may hold values from 0 to 15, as said below
- cover_freqs: int32 [512], P(('windows', 'tiles')), parts along dimension 0, may hold values from 0 to 7
Outputs:
- residual: float32 [16, 2, 2048, 128], P('windows', None, 'tiles'), parts along dimension 0
- gradient: bfloat16 [512, 2, 128, 128], P(('windows', 'tiles')), parts along dimension 0
There are 2 independent parts, one for each index of `windows`. A program takes and returns all parts, laid end to end along the dimension named above; an argument that names none is the same for every part. Nothing has to cross between parts.
Inputs may be any that keep to these rules, and one draw needn't show every extreme that they name: `cover_rows`: among the 16 entries of one column block no row block appears more than 2 times, exactly 12 distinct row blocks appear, one row block appears 2 times in every column block, and together with cover_freqs the entries of one column block name distinct (row block, frequency) pairs.
All inputs are finite; a program needn't handle non-finite values.
Results may differ from a plain program's by a relative error of at most 0.0053.
Values may be sent and summed in bfloat16 or wider, within the bound.
No kernel may reach another device: no remote copies, remote signals or barrier semaphores. Data moves between devices by JAX's collectives and lax.ppermute only.
A program may use at most 128 MiB of HBM per device.

v0:
```python
import jax
import jax.numpy as jnp
from jax import lax
from jax.sharding import PartitionSpec as P

CAP = 2


def complex_product(left, right):
    real_in = left[:, 0]
    imag_in = left[:, 1]
    stacked = jnp.stack(
        [jnp.stack([real_in, -imag_in], axis=1), jnp.stack([imag_in, real_in], axis=1)], axis=1
    )
    return jnp.einsum("sxyab,sybp->sxap", stacked, right, preferred_element_type=jnp.float32)


def shot_gradient(rows_res, rows_src):
    scale = 1.0 / rows_src.shape[-1]
    src_real = rows_src[:, 0]
    src_imag = rows_src[:, 1]
    stacked = jnp.stack(
        [jnp.stack([src_real, src_imag], axis=1), jnp.stack([-src_imag, src_real], axis=1)], axis=1
    )
    total = jnp.einsum("kyap,kxybp->kxab", rows_res, stacked, preferred_element_type=jnp.float32)
    return (-total * scale).astype(jnp.bfloat16)


def per_device(data, wavelet, panel_block, tiles, cover_rows, cover_freqs):
    freq_count = data.shape[0]
    block_rows = data.shape[2]
    shots = data.shape[3]
    slots = tiles.shape[0]
    peers = lax.axis_size("tiles")
    device = lax.axis_index("tiles")
    identity = (jnp.arange(block_rows)[:, None] == jnp.arange(shots)[None, :]).astype(jnp.float32)
    at_panel = (device == panel_block[0]).astype(jnp.float32)
    source_re = -data[:, 0].astype(jnp.float32) + at_panel * wavelet[:, 0, None, None] * identity
    source_im = -data[:, 1].astype(jnp.float32) + at_panel * wavelet[:, 1, None, None] * identity
    source = jnp.stack([source_re, source_im], axis=1).astype(jnp.bfloat16)
    slot_src = source[cover_freqs]
    earlier = jnp.arange(slots)[:, None] > jnp.arange(slots)[None, :]
    same_row = cover_rows[:, None] == cover_rows[None, :]
    position = jnp.sum(jnp.logical_and(same_row, earlier), axis=1)
    target = cover_rows * CAP + position
    freq_onehot = (cover_freqs[:, None] == jnp.arange(freq_count)[None, :]).astype(jnp.bfloat16)
    freq_values = jnp.arange(freq_count).astype(jnp.float32)

    def place(values):
        buffer = jnp.zeros((peers * CAP,) + values.shape[1:], values.dtype).at[target].set(values)
        return buffer.reshape((peers, CAP) + values.shape[1:])

    parts = complex_product(tiles, slot_src).astype(jnp.bfloat16)
    got_parts, got_freqs = (
        lax.all_to_all(place(parts), "tiles", split_axis=0, concat_axis=0, tiled=True),
        lax.all_to_all(place(freq_onehot), "tiles", split_axis=0, concat_axis=0, tiled=True),
    )
    predicted = jnp.einsum(
        "ncf,ncxbp->fxbp", got_freqs, got_parts, preferred_element_type=jnp.float32
    )
    residual = data.astype(jnp.float32) - predicted
    res_rounded = residual.astype(jnp.bfloat16)
    slot_index = jnp.sum(got_freqs.astype(jnp.float32) * freq_values[None, None, :], axis=2).astype(
        jnp.int32
    )
    send_back = res_rounded[slot_index]
    returned = lax.all_to_all(send_back, "tiles", split_axis=0, concat_axis=0, tiled=True)
    slot_res = returned.reshape((peers * CAP,) + returned.shape[2:])[target]
    gradient = shot_gradient(slot_res, slot_src)
    return (residual, gradient)


def solution(mesh):
    in_specs = (
        P("windows", None, "tiles", None),
        P(),
        P(),
        P(("windows", "tiles"), None, None, None),
        P(("windows", "tiles")),
        P(("windows", "tiles")),
    )
    out_specs = (P("windows", None, "tiles", None), P(("windows", "tiles"), None, None, None))
    return jax.shard_map(
        per_device, mesh=mesh, in_specs=in_specs, out_specs=out_specs, check_vma=False
    )
```

profile of v0, /device:TPU:15, one launch (start us, length us, event | category | flops | bytes accessed | tf_op | source)
XLA Modules:
  0.0 138.8 jit_solution(14115497230437427584)
XLA Ops:
  0.7 0.9 convert_reduce_fusion
  1.6 0.7 compare_select_fusion.2
  2.2 1.4 scatter_custom_fusion
  3.6 6.6 %all-to-all-start = ((bf16[16,2,8]{2,1,0:T(2,128)(2,1)}), bf16[16,2,8]{2,1,0:T(2,128)(2,1)S(1)}, u32[]{:S(2)}, u32[]{:S(2)}) async-start(bf16[16,2,8]{2,1,0:T(2,128)(2,1)} %bitcast), calls=%async_computation | async-start | bytes 16384 | tf_op jit(solution)/shard_map/all_to_all | solution.py:56
  10.2 0.7 compare_select_fusion.1
  11.5 1.3 slice_negate_fusion.1
  12.9 0.2 add_convert_fusion.1
  13.2 0.7 gather_fusion
  14.1 1.7 %bitcast_convert_fusion = bf16[16,2,128,128]{3,2,1,0:T(8,128)(2,1)} fusion(bf16[16,1,2,128,128]{4,3,2,1,0:T(8,128)(2,1)S(1)} %get-tuple-element.22, bf16[16,1,2,128,128]{4,3,2,1,0:T(8,128)(2,1)S(1)} %get-tuple-element.21, bf16[16,2,128,128]{3,2,1,0:T(8,128)(2,1)S(1)} %gather_fusion), kind=kOutput, calls=%fused_computation.16 | convolution fusion | flops 270008320 | bytes 4194304 | tf_op jit(solution)/shard_map/sxyab,sybp->sxap/dot_general | solution.py:15
  15.7 0.5 broadcast_in_dim.10
  16.2 2.3 %scatter_fusion = bf16[32,2,128,128]{3,2,1,0:T(8,128)(2,1)S(1)} fusion(bf16[32,2,128,128]{3,2,1,0:T(8,128)(2,1)S(1)} %broadcast_in_dim.10, s32[16]{0:T(128)S(1)} %compare_select_fusion.2, bf16[16,2,128,128]{3,2,1,0:T(8,128)(2,1)} %bitcast_convert_fusion), kind=kCustom, calls=%fused_computation.4 | custom fusion | bytes 3145792 | tf_op jit(solution)/shard_map/scatter | solution.py:50
  18.5 3.5 %copy.57 = bf16[16,2,2,128,128]{4,1,3,2,0:T(2,128)(2,1)} copy(bf16[16,2,2,128,128]{4,3,2,1,0:T(8,128)(2,1)S(1)} %bitcast.55) | data formatting | bytes 4194304 | tf_op jit(solution)/shard_map/reshape | solution.py:51
  22.0 6.0 %all-to-all-start.1 = ((bf16[16,2,2,128,128]{4,1,3,2,0:T(2,128)(2,1)}), bf16[16,2,2,128,128]{4,1,3,2,0:T(2,128)(2,1)S(1)}, u32[]{:S(2)}, u32[]{:S(2)}) async-start(bf16[16,2,2,128,128]{4,1,3,2,0:T(2,128)(2,1)} %copy.57), calls=%async_computation.1 | async-start | bytes 4194304 | tf_op jit(solution)/shard_map/all_to_all | solution.py:55
  28.5 47.0 %all-to-all-done.1 = bf16[16,2,2,128,128]{4,1,3,2,0:T(2,128)(2,1)S(1)} async-done(((bf16[16,2,2,128,128]{4,1,3,2,0:T(2,128)(2,1)}), bf16[16,2,2,128,128]{4,1,3,2,0:T(2,128)(2,1)S(1)}, u32[]{:S(2)}, u32[]{:S(2)}) %all-to-all-start.1) | async-done | bytes 2097184 | tf_op jit(solution)/shard_map/all_to_all | solution.py:55
  75.5 3.5 %fusion.37 = (bf16[8,2,128,128]{3,0,2,1:T(8,128)(2,1)S(1)}, f32[8,2,128,128]{3,0,2,1:T(8,128)}) fusion(bf16[16,2,2,128,128]{4,1,3,2,0:T(2,128)(2,1)S(1)} %all-to-all-done.1, bf16[16,2,8,1,1]{2,1,0,4,3:T(2,128)(2,1)S(1)} %bitcast.58, bf16[8,2,128,128]{3,2,1,0:T(8,128)(2,1)} %param.6), kind=kOutput, calls=%fused_computation.55 | convolution fusion | flops 17563648 | bytes 4194816 | tf_op jit(solution)/shard_map/ncf,ncxbp->fxbp/dot_general | solution.py:58
  79.1 2.2 %gather_fusion.1 = bf16[32,2,128,128]{3,2,1,0:T(8,128)(2,1)} fusion(bf16[8,2,128,128]{3,2,1,0:T(8,128)(2,1)S(1)} %copy.63, s32[1024]{0:T(1024)S(1)} %pad_clamp_fusion.1), kind=kCustom, calls=%fused_computation.1 | custom fusion | bytes 4194432 | tf_op jit(solution)/shard_map/gather | solution.py:66
  81.2 4.9 %all-to-all-start.2 = ((bf16[16,2,2,128,128]{4,3,2,1,0:T(8,128)(2,1)}), bf16[16,2,2,128,128]{4,3,2,1,0:T(8,128)(2,1)S(1)}, u32[]{:S(2)}, u32[]{:S(2)}) async-start(bf16[16,2,2,128,128]{4,3,2,1,0:T(8,128)(2,1)} %bitcast.19), calls=%async_computation.2 | async-start | bytes 4194304 | tf_op jit(solution)/shard_map/all_to_all | solution.py:67
  86.3 1.1 maximum_bitcast_fusion.2
  87.4 0.2 copy-done
  87.6 1.2 copy.64
  88.7 44.8 %all-to-all-done.2 = bf16[16,2,2,128,128]{4,3,2,1,0:T(8,128)(2,1)S(1)} async-done(((bf16[16,2,2,128,128]{4,3,2,1,0:T(8,128)(2,1)}), bf16[16,2,2,128,128]{4,3,2,1,0:T(8,128)(2,1)S(1)}, u32[]{:S(2)}, u32[]{:S(2)}) %all-to-all-start.2) | async-done | bytes 2097184 | tf_op jit(solution)/shard_map/all_to_all | solution.py:67
  133.6 1.6 %gather_fusion.2 = bf16[16,2,128,128]{3,2,1,0:T(8,128)(2,1)} fusion(bf16[32,2,128,128]{3,2,1,0:T(8,128)(2,1)S(1)} %bitcast.56, s32[1024]{0:T(1024)S(1)} %pad_clamp_fusion), kind=kCustom, calls=%fused_computation.2 | custom fusion | bytes 2097216 | tf_op jit(solution)/shard_map/gather | solution.py:68
  135.2 2.2 %fusion.19 = bf16[16,2,128,128]{2,3,1,0:T(8,128)(2,1)S(1)} fusion(bf16[16,1,2,128,128]{4,3,2,1,0:T(8,128)(2,1)} %maximum_bitcast_fusion.2, bf16[16,1,2,128,128]{4,3,2,1,0:T(8,128)(2,1)S(1)} %bitcast.57, bf16[16,2,128,128]{3,2,1,0:T(8,128)(2,1)} %gather_fusion.2), kind=kOutput, calls=%fused_computation.20 | convolution fusion | flops 271056896 | bytes 4194304 | tf_op jit(solution)/shard_map/kyap,kxybp->kxab/dot_general | solution.py:25
  137.5 1.3 copy.65
  (22 shorter events, 0.8 us)
Async XLA Ops:
  0.6 12.2 %copy-start.2 = (f32[8,2]{0,1:T(2,128)S(1)}, f32[8,2]{0,1:T(2,128)}, u32[]{:S(2)}) copy-start(f32[8,2]{0,1:T(2,128)} %param.7) | copy-start | bytes 196
  0.6 12.2 %copy-start.1 = (bf16[8,2,128,128]{3,2,1,0:T(8,128)(2,1)S(1)}, bf16[8,2,128,128]{3,2,1,0:T(8,128)(2,1)}, u32[]{:S(2)}) copy-start(bf16[8,2,128,128]{3,2,1,0:T(8,128)(2,1)} %param.6) | copy-start | bytes 1572868
  3.6 18.5 %all-to-all-start = ((bf16[16,2,8]{2,1,0:T(2,128)(2,1)}), bf16[16,2,8]{2,1,0:T(2,128)(2,1)S(1)}, u32[]{:S(2)}, u32[]{:S(2)}) async-start(bf16[16,2,8]{2,1,0:T(2,128)(2,1)} %bitcast), calls=%async_computation | async-start | bytes 16384 | tf_op jit(solution)/shard_map/all_to_all | solution.py:56
  22.0 53.4 %all-to-all-start.1 = ((bf16[16,2,2,128,128]{4,1,3,2,0:T(2,128)(2,1)}), bf16[16,2,2,128,128]{4,1,3,2,0:T(2,128)(2,1)S(1)}, u32[]{:S(2)}, u32[]{:S(2)}) async-start(bf16[16,2,2,128,128]{4,1,3,2,0:T(2,128)(2,1)} %copy.57), calls=%async_computation.1 | async-start | bytes 4194304 | tf_op jit(solution)/shard_map/all_to_all | solution.py:55
  81.2 52.3 %all-to-all-start.2 = ((bf16[16,2,2,128,128]{4,3,2,1,0:T(8,128)(2,1)}), bf16[16,2,2,128,128]{4,3,2,1,0:T(8,128)(2,1)S(1)}, u32[]{:S(2)}, u32[]{:S(2)}) async-start(bf16[16,2,2,128,128]{4,3,2,1,0:T(8,128)(2,1)} %bitcast.19), calls=%async_computation.2 | async-start | bytes 4194304 | tf_op jit(solution)/shard_map/all_to_all | solution.py:67
  86.1 1.4 %copy-start = (f32[8,2,128,128]{3,0,2,1:T(8,128)S(1)}, f32[8,2,128,128]{3,0,2,1:T(8,128)}, u32[]{:S(2)}) copy-start(f32[8,2,128,128]{3,0,2,1:T(8,128)} %get-tuple-element.26) | copy-start | bytes 3145732
where the time goes:
time: 139 us
  waiting for transfers between devices  91.8 us (66%)
  starting transfers between devices  17.5 us (13%)
  local copies, waits for them, and re-layouts  13.9 us (10%)
  matrix products  7.41 us (5%)
  other arithmetic  6.69 us (5%)
  between operations  1.45 us (1%)
    all_to_all x1, waiting for transfers between devices, per_device(): lax.all_to_all(place(parts), 'tiles', split_axis=0, concat_axis=0, tiled=...  47 us
    all_to_all x1, waiting for transfers between devices, per_device(): lax.all_to_all(send_back, 'tiles', split_axis=0, concat_axis=0, tiled=True)  44.8 us
    all_to_all x1, starting transfers between devices, per_device(): lax.all_to_all(place(freq_onehot), 'tiles', split_axis=0, concat_axis=0,...  6.55 us
    all_to_all x1, starting transfers between devices, per_device(): lax.all_to_all(place(parts), 'tiles', split_axis=0, concat_axis=0, tiled=...  6.02 us
    all_to_all x1, starting transfers between devices, per_device(): lax.all_to_all(send_back, 'tiles', split_axis=0, concat_axis=0, tiled=True)  4.91 us
    reshape x1, local copies, waits for them, and re-layouts, place(): return buffer.reshape((peers, CAP) + values.shape[1:])  3.52 us
    dot_general x1, matrix products, per_device(): jnp.einsum('ncf,ncxbp->fxbp', got_freqs, got_parts, preferred_element_typ...  3.48 us
    unnamed x9, local copies, waits for them, and re-layouts  2.8 us
  transfers between devices with their start and end apart: 3, of which 2 were waited for; matrix products, arithmetic and copies ran while one was open for 10% of the time, Pallas kernels for 0%

commit v1 on v0

v1 whole, which is shorter than its diff:
```python
import functools

import jax
import jax.numpy as jnp
from jax import lax
from jax.experimental import pallas as pl
from jax.experimental.pallas import tpu as pltpu
from jax.sharding import PartitionSpec as P

GROUP = 8
CHUNKS = 2
BF16 = jnp.bfloat16
F32 = jnp.float32
VMEM = pl.BlockSpec(memory_space=pltpu.VMEM)
SMEM = pl.BlockSpec(memory_space=pltpu.SMEM)


def call(kernel, name, out_shape, scratch=(), specs=None, flops=0, moved=1 << 20):
    return pl.pallas_call(
        kernel,
        name=name,
        out_shape=out_shape,
        in_specs=specs,
        out_specs=jax.tree.map(lambda _: VMEM, out_shape),
        scratch_shapes=list(scratch),
        cost_estimate=pl.CostEstimate(flops=flops, bytes_accessed=moved, transcendentals=0),
        compiler_params=pltpu.CompilerParams(vmem_limit_bytes=40 * 1024 * 1024),
    )


def local_index():
    return lax.rem(lax.axis_index("tiles"), GROUP)


def group_index():
    return lax.div(lax.axis_index("tiles"), GROUP)


def pack(real, imag):
    return jnp.concatenate([real, imag], axis=0).astype(BF16)


def slices_kernel(data, rows, freqs, *outs):
    outs, wide = outs[:-1], outs[-1]
    wide[...] = data[...].astype(F32)
    local = local_index()
    freq_count, _, block, shots = data.shape
    chunk = block // CHUNKS
    piece = chunk // GROUP
    slots = rows.shape[0]
    for k in range(GROUP):
        start = (local ^ k) * piece
        for c in range(CHUNKS):
            at = pl.ds(pl.multiple_of(c * chunk + start, piece), piece)
            for f in range(freq_count):
                outs[k][c * freq_count + f] = pack(wide[f, 0, at, :], wide[f, 1, at, :])
    lists = jnp.zeros((2 * slots, shots), F32)
    line = lax.broadcasted_iota(jnp.int32, (2 * slots, shots), 0)

    def put(t, lists):
        lists = jnp.where(line == t, rows[t].astype(F32), lists)
        return jnp.where(line == slots + t, freqs[t].astype(F32), lists)

    lists = lax.fori_loop(0, slots, put, lists)
    height = 2 * piece
    for b in range(2 * slots // height):
        for k in range(GROUP):
            outs[k][CHUNKS * freq_count + b] = lists[b * height : (b + 1) * height].astype(BF16)


def parts_kernel(data, wavelet, panel, tiles, freqs, source, *outs_scratch):
    outs, product = outs_scratch[:-1], outs_scratch[-1]
    local = local_index()
    freq_count, _, block, shots = data.shape
    chunk = block // CHUNKS
    piece = chunk // GROUP
    at_panel = (lax.axis_index("tiles") == panel[0]).astype(F32)
    identity = (
        lax.broadcasted_iota(jnp.int32, (block, shots), 0)
        == lax.broadcasted_iota(jnp.int32, (block, shots), 1)
    ).astype(F32) * at_panel
    for f in range(freq_count):
        real = -data[f, 0].astype(F32) + wavelet[f, 0] * identity
        imag = -data[f, 1].astype(F32) + wavelet[f, 1] * identity
        source[f, :block, :shots] = real.astype(BF16)
        source[f, :block, shots:] = imag.astype(BF16)
        source[f, block:, :shots] = (-imag).astype(BF16)
        source[f, block:, shots:] = real.astype(BF16)

    def one(t, carry):
        left = jnp.concatenate([tiles[t, 0], tiles[t, 1]], axis=1)
        product[...] = jnp.dot(left, source[freqs[t]], preferred_element_type=F32)
        for c in range(CHUNKS):
            for k in range(GROUP):
                at = pl.ds(pl.multiple_of(c * chunk + (local ^ k) * piece, piece), piece)
                outs[c * GROUP + k][t] = pack(product[at, :shots], product[at, shots:])
        return carry

    lax.fori_loop(0, tiles.shape[0], one, 0)


def combine_kernel(freq_count, index, *refs):
    parts, own, sends, total = refs[:GROUP], refs[GROUP], refs[GROUP + 1 : -1], refs[-1]
    slots = parts[0].shape[0]
    group = group_index()
    span = GROUP * freq_count

    total[...] = jnp.zeros_like(total)
    for k in range(GROUP):

        def add(t, carry, k=k):
            at = index[k, t]
            total[at] += parts[k][t].astype(F32)
            return carry

        lax.fori_loop(0, slots, add, 0, unroll=4)
    own[...] = total[pl.ds(group * span, span)]
    for q, send in enumerate(sends, 1):
        send[...] = total[pl.ds((group ^ q) * span, span)].astype(BF16)


def residual_kernel(freq_count, at_chunk, own, *refs):
    count = len(refs) - 2 * GROUP - 1
    got, data = refs[:count], refs[count : count + GROUP]
    rounded, back = refs[count + GROUP], refs[count + GROUP + 1 :]
    local = local_index()
    for k in range(GROUP):
        at = pl.ds((local ^ k) * freq_count, freq_count)
        predicted = own[at]
        for ref in got:
            predicted += ref[at].astype(F32)
        values = data[k][at_chunk * freq_count : (at_chunk + 1) * freq_count].astype(F32)
        rounded[at] = (values - predicted).astype(BF16)
        back[k][...] = predicted.astype(BF16)


def spread_kernel(freq_count, index, *refs):
    outs, table = refs[-GROUP - 1 : -1], refs[-1]
    have = refs[: -GROUP - 1]
    group = group_index()
    span = GROUP * freq_count
    for q, ref in enumerate(have):
        table[pl.ds((group ^ q) * span, span)] = ref[...]
    for k in range(GROUP):

        def take(t, carry, k=k):
            outs[k][t] = table[index[k, t]]
            return carry

        lax.fori_loop(0, outs[0].shape[0], take, 0, unroll=4)


def gradient_kernel(data, source, freqs, *refs):
    slices, back = refs[: CHUNKS * GROUP], refs[CHUNKS * GROUP : 2 * CHUNKS * GROUP]
    residual, gradient, left = refs[2 * CHUNKS * GROUP :]
    local = local_index()
    freq_count, _, block, shots = data.shape
    chunk = block // CHUNKS
    piece = chunk // GROUP
    scale = 1.0 / shots
    residual[...] = data[...].astype(F32)
    for c in range(CHUNKS):
        for k in range(GROUP):
            at = pl.ds(pl.multiple_of(c * chunk + (local ^ k) * piece, piece), piece)
            for f in range(freq_count):
                predicted = back[c * GROUP + k][f].astype(F32)
                residual[f, 0, at, :] -= predicted[:piece]
                residual[f, 1, at, :] -= predicted[piece:]

    def one(t, carry):
        for c in range(CHUNKS):
            for k in range(GROUP):
                at = pl.ds(pl.multiple_of(c * chunk + (local ^ k) * piece, piece), piece)
                values = slices[c * GROUP + k][t].astype(F32)
                left[at, :shots] = values[:piece]
                left[at, shots:] = values[piece:]
        total = lax.dot_general(
            left[...].astype(BF16),
            source[freqs[t]],
            (((1,), (1,)), ((), ())),
            preferred_element_type=F32,
        )
        total = (-total * scale).astype(BF16)
        gradient[t, 0] = total[:, :block]
        gradient[t, 1] = total[:, block:]
        return carry

    lax.fori_loop(0, gradient.shape[0], one, 0)


def per_device(data, wavelet, panel_block, tiles, cover_rows, cover_freqs):
    freq_count, _, block, shots = data.shape
    slots = tiles.shape[0]
    peers = lax.axis_size("tiles")
    groups = peers // GROUP
    height = 2 * block // (CHUNKS * GROUP)
    span = GROUP * freq_count

    def shape(count, kind=BF16):
        return jax.ShapeDtypeStruct((count, height, shots), kind)

    def swap(value, distance):
        pairs = [(i, i ^ distance) for i in range(peers)]
        return lax.ppermute(value, "tiles", pairs)

    def exchange(values):
        got = {k: swap(values[k], k) for k in (6, 4, 7, 5, 2, 3, 1)}
        got[0] = values[0]
        return [got[k] for k in range(GROUP)]

    def across(values):
        return [swap(value, (q + 1) * GROUP) for q, value in enumerate(values)]

    lists = 2 * slots // height
    data_out = call(
        slices_kernel,
        "data_slices",
        [shape(CHUNKS * freq_count + lists)] * GROUP,
        scratch=[pltpu.VMEM(data.shape, F32)],
        specs=[VMEM, SMEM, SMEM],
    )(data, cover_rows, cover_freqs)
    data_in = exchange(data_out)

    source, *parts = call(
        parts_kernel,
        "parts",
        [jax.ShapeDtypeStruct((freq_count, 2 * block, 2 * shots), BF16)]
        + [shape(slots)] * (CHUNKS * GROUP),
        scratch=[pltpu.VMEM((block, 2 * shots), F32)],
        specs=[VMEM, SMEM, SMEM, VMEM, SMEM],
    )(data, wavelet, panel_block, tiles, cover_freqs)

    cover = jnp.stack([x[CHUNKS * freq_count :, :, 0].reshape(2, slots) for x in data_in])
    cover = cover.astype(jnp.int32)
    index = cover[:, 0] * freq_count + cover[:, 1]

    arrived = [exchange(parts[c * GROUP : (c + 1) * GROUP]) for c in range(CHUNKS)]
    sums = []
    for c in range(CHUNKS):
        own, *sends = call(
            functools.partial(combine_kernel, freq_count),
            "combine",
            [shape(span, F32)] + [shape(span)] * (groups - 1),
            scratch=[pltpu.VMEM((peers * freq_count, height, shots), F32)],
            specs=[SMEM] + [VMEM] * GROUP,
        )(index, *arrived[c])
        sums.append((own, across(sends)))
    rounded, back = [], []
    for c in range(CHUNKS):
        own, got = sums[c]
        mine, *predicted = call(
            functools.partial(residual_kernel, freq_count, c),
            "residual_slices",
            [shape(span)] + [shape(freq_count)] * GROUP,
            specs=[VMEM] * (1 + len(got) + GROUP),
        )(own, *got, *data_in)
        rounded.append([mine] + across([mine] * (groups - 1)))
        back.append(predicted)
    slices = []
    for c in range(CHUNKS):
        out = call(
            functools.partial(spread_kernel, freq_count),
            "spread",
            [shape(slots)] * GROUP,
            scratch=[pltpu.VMEM((peers * freq_count, height, shots), BF16)],
            specs=[SMEM] + [VMEM] * groups,
        )(index, *rounded[c])
        slices += exchange(out)
    returned = []
    for c in range(CHUNKS):
        returned += exchange(back[c])
    return call(
        gradient_kernel,
        "gradient",
        [
            jax.ShapeDtypeStruct(data.shape, F32),
            jax.ShapeDtypeStruct(tiles.shape, BF16),
        ],
        scratch=[pltpu.VMEM((block, 2 * shots), F32)],
        specs=[VMEM, VMEM, SMEM] + [VMEM] * (2 * CHUNKS * GROUP),
    )(data, source, cover_freqs, *slices, *returned)


def solution(mesh):
    in_specs = (
        P("windows", None, "tiles", None),
        P(),
        P(),
        P(("windows", "tiles"), None, None, None),
        P(("windows", "tiles")),
        P(("windows", "tiles")),
    )
    out_specs = (P("windows", None, "tiles", None), P(("windows", "tiles"), None, None, None))
    return jax.shard_map(
        lambda *args: tuple(per_device(*args)),
        mesh=mesh,
        in_specs=in_specs,
        out_specs=out_specs,
        check_vma=False,
    )
```

time: 139 us -> 122 us (0.88)
  the two profiles are of different devices: /device:TPU:15 before, /device:TPU:0 now
where the time goes in v1:
time: 122 us
  starting transfers between devices  55 us (45%)
  waiting for transfers between devices  45.4 us (37%)
  Pallas kernels  14.9 us (12%)
  local copies, waits for them, and re-layouts  5 us (4%)
  between operations  1.52 us (1%)
    ppermute x53, starting transfers between devices, swap(): return lax.ppermute(value, 'tiles', pairs)  55 us
    ppermute x53, waiting for transfers between devices, swap(): return lax.ppermute(value, 'tiles', pairs)  45.4 us
    pallas_call x1, Pallas kernels, per_device(): call(gradient_kernel, 'gradient', [jax.ShapeDtypeStruct(data.shape, F32),...  5.25 us
    unnamed x22, local copies, waits for them, and re-layouts  4.3 us
    pallas_call x1, Pallas kernels, per_device(): call(parts_kernel, 'parts', [jax.ShapeDtypeStruct((freq_count, 2 * block,...  3.78 us
    pallas_call x2, Pallas kernels, per_device(): call(functools.partial(combine_kernel, freq_count), 'combine', [shape(spa...  2.61 us
  transfers between devices with their start and end apart: 53, of which 14 were waited for; matrix products, arithmetic and copies ran while one was open for 1% of the time, Pallas kernels for 7%

profile of v1, /device:TPU:0, one launch (start us, length us, event | category | flops | bytes accessed | tf_op | source)
XLA Modules:
  0.0 121.8 jit_solution(14412344922426897970)
XLA Ops:
  4.4 2.6 %collective-permute-start.1 = (bf16[18,16,128]{2,1,0:T(8,128)(2,1)S(1)}, bf16[18,16,128]{2,1,0:T(8,128)(2,1)S(1)}, u32[]{:S(2)}, u32[]{:S(2)}) collective-permute-start(bf16[18,16,128]{2,1,0:T(8,128)(2,1)S(1)} %get-tuple-element.68), channel_id=1, source_target_pairs={{0,2},{1,3},{2,0},{3,1},{4,6},{5,7},{6,4},{7,5},{8,10},{9,11},{10,... | collective-permute-start | bytes 221192 | tf_op jit(solution)/shard_map/ppermute | solution.py:204
  7.0 1.8 %collective-permute-start.3 = (bf16[18,16,128]{2,1,0:T(8,128)(2,1)S(1)}, bf16[18,16,128]{2,1,0:T(8,128)(2,1)S(1)}, u32[]{:S(2)}, u32[]{:S(2)}) collective-permute-start(bf16[18,16,128]{2,1,0:T(8,128)(2,1)S(1)} %get-tuple-element.70), channel_id=1, source_target_pairs={{0,4},{1,5},{2,6},{3,7},{4,0},{5,1},{6,2},{7,3},{8,12},{9,13},{10,... | collective-permute-start | bytes 221192 | tf_op jit(solution)/shard_map/ppermute | solution.py:204
  11.5 3.8 %parts.1 = (bf16[8,256,256]{2,1,0:T(8,128)(2,1)S(1)}, bf16[16,16,128]{2,1,0:T(8,128)(2,1)S(1)}, bf16[16,16,128]{2,1,0:T(8,128)(2,1)S(1)}, bf16[16,16,128]{2,1,0:...) custom-call(bf16[8,2,128,128]{3,2,1,0:T(8,128)(2,1)S(1)} %copy-done., ...), custom_call_target="tpu_custom_call" | custom-call | bytes 1048576 | tf_op jit(solution)/shard_map/parts/pallas_call | solution.py:224
  15.3 2.7 %collective-permute-start.5 = (bf16[18,16,128]{2,1,0:T(8,128)(2,1)S(1)}, bf16[18,16,128]{2,1,0:T(8,128)(2,1)S(1)}, u32[]{:S(2)}, u32[]{:S(2)}) collective-permute-start(bf16[18,16,128]{2,1,0:T(8,128)(2,1)S(1)} %get-tuple-element.72), channel_id=1, source_target_pairs={{0,6},{1,7},{2,4},{3,5},{4,2},{5,3},{6,0},{7,1},{8,14},{9,15},{10,... | collective-permute-start | bytes 221192 | tf_op jit(solution)/shard_map/ppermute | solution.py:204
  18.8 1.7 %collective-permute-start.8 = (bf16[16,16,128]{2,1,0:T(8,128)(2,1)S(1)}, bf16[16,16,128]{2,1,0:T(8,128)(2,1)S(1)}, u32[]{:S(2)}, u32[]{:S(2)}) collective-permute-start(bf16[16,16,128]{2,1,0:T(8,128)(2,1)S(1)} %get-tuple-element.76), channel_id=1, source_target_pairs={{0,2},{1,3},{2,0},{3,1},{4,6},{5,7},{6,4},{7,5},{8,10},{9,11},{10,... | collective-permute-start | bytes 196616 | tf_op jit(solution)/shard_map/ppermute | solution.py:204
  20.9 1.8 %collective-permute-start.10 = (bf16[16,16,128]{2,1,0:T(8,128)(2,1)S(1)}, bf16[16,16,128]{2,1,0:T(8,128)(2,1)S(1)}, u32[]{:S(2)}, u32[]{:S(2)}) collective-permute-start(bf16[16,16,128]{2,1,0:T(8,128)(2,1)S(1)} %get-tuple-element.78), channel_id=1, source_target_pairs={{0,4},{1,5},{2,6},{3,7},{4,0},{5,1},{6,2},{7,3},{8,12},{9,13},{10,... | collective-permute-start | bytes 196616 | tf_op jit(solution)/shard_map/ppermute | solution.py:204
  23.8 1.8 %collective-permute-start.12 = (bf16[16,16,128]{2,1,0:T(8,128)(2,1)S(1)}, bf16[16,16,128]{2,1,0:T(8,128)(2,1)S(1)}, u32[]{:S(2)}, u32[]{:S(2)}) collective-permute-start(bf16[16,16,128]{2,1,0:T(8,128)(2,1)S(1)} %get-tuple-element.80), channel_id=1, source_target_pairs={{0,6},{1,7},{2,4},{3,5},{4,2},{5,3},{6,0},{7,1},{8,14},{9,15},{10,... | collective-permute-start | bytes 196616 | tf_op jit(solution)/shard_map/ppermute | solution.py:204
  26.8 1.5 %collective-permute-start.24 = (bf16[16,16,128]{2,1,0:T(8,128)(2,1)S(1)}, bf16[16,16,128]{2,1,0:T(8,128)(2,1)S(1)}, u32[]{:S(2)}, u32[]{:S(2)}) collective-permute-start(bf16[16,16,128]{2,1,0:T(8,128)(2,1)S(1)} %get-tuple-element.95), channel_id=1, source_target_pairs={{0,2},{1,3},{2,0},{3,1},{4,6},{5,7},{6,4},{7,5},{8,10},{9,11},{10,... | collective-permute-start | bytes 196616 | tf_op jit(solution)/shard_map/ppermute | solution.py:204
  29.8 1.7 %collective-permute-start.26 = (bf16[16,16,128]{2,1,0:T(8,128)(2,1)S(1)}, bf16[16,16,128]{2,1,0:T(8,128)(2,1)S(1)}, u32[]{:S(2)}, u32[]{:S(2)}) collective-permute-start(bf16[16,16,128]{2,1,0:T(8,128)(2,1)S(1)} %get-tuple-element.97), channel_id=1, source_target_pairs={{0,4},{1,5},{2,6},{3,7},{4,0},{5,1},{6,2},{7,3},{8,12},{9,13},{10,... | collective-permute-start | bytes 196616 | tf_op jit(solution)/shard_map/ppermute | solution.py:204
  33.1 1.5 %collective-permute-start.29 = (bf16[16,16,128]{2,1,0:T(8,128)(2,1)S(1)}, bf16[16,16,128]{2,1,0:T(8,128)(2,1)S(1)}, u32[]{:S(2)}, u32[]{:S(2)}) collective-permute-start(bf16[16,16,128]{2,1,0:T(8,128)(2,1)S(1)} %get-tuple-element.100), channel_id=1, source_target_pairs={{0,7},{1,6},{2,5},{3,4},{4,3},{5,2},{6,1},{7,0},{8,15},{9,14},{10,... | collective-permute-start | bytes 196616 | tf_op jit(solution)/shard_map/ppermute | solution.py:204
  35.9 2.6 %collective-permute-start.14 = (bf16[64,16,128]{2,1,0:T(8,128)(2,1)S(1)}, bf16[64,16,128]{2,1,0:T(8,128)(2,1)S(1)}, u32[]{:S(2)}, u32[]{:S(2)}) collective-permute-start(bf16[64,16,128]{2,1,0:T(8,128)(2,1)S(1)} %get-tuple-element.83), channel_id=1, source_target_pairs={{0,8},{1,9},{2,10},{3,11},{4,12},{5,13},{6,14},{7,15},{8,0},{9,1},... | collective-permute-start | bytes 786440 | tf_op jit(solution)/shard_map/ppermute | solution.py:204
  39.9 2.5 %collective-permute-start.30 = (bf16[64,16,128]{2,1,0:T(8,128)(2,1)S(1)}, bf16[64,16,128]{2,1,0:T(8,128)(2,1)S(1)}, u32[]{:S(2)}, u32[]{:S(2)}) collective-permute-start(bf16[64,16,128]{2,1,0:T(8,128)(2,1)S(1)} %get-tuple-element.102), channel_id=1, source_target_pairs={{0,8},{1,9},{2,10},{3,11},{4,12},{5,13},{6,14},{7,15},{8,0},{9,1},... | collective-permute-start | bytes 786440 | tf_op jit(solution)/shard_map/ppermute | solution.py:204
  42.3 14.8 %collective-permute-done.14.refs_0_ = bf16[64,16,128]{2,1,0:T(8,128)(2,1)S(1)} collective-permute-done((bf16[64,16,128]{2,1,0:T(8,128)(2,1)S(1)}, bf16[64,16,128]{2,1,0:T(8,128)(2,1)S(1)}, u32[]{:S(2)}, u32[]{:S(2)}) %collective-permute-start.14) | collective-permute-done | bytes 262176 | tf_op jit(solution)/shard_map/ppermute | solution.py:204
  57.3 11.0 %collective-permute-done.30.refs_0_ = bf16[64,16,128]{2,1,0:T(8,128)(2,1)S(1)} collective-permute-done((bf16[64,16,128]{2,1,0:T(8,128)(2,1)S(1)}, bf16[64,16,128]{2,1,0:T(8,128)(2,1)S(1)}, u32[]{:S(2)}, u32[]{:S(2)}) %collective-permute-start.30) | collective-permute-done | bytes 262176 | tf_op jit(solution)/shard_map/ppermute | solution.py:204
  70.5 3.7 %collective-permute-start.42 = (bf16[8,16,128]{2,1,0:T(8,128)(2,1)S(1)}, bf16[8,16,128]{2,1,0:T(8,128)(2,1)S(1)}, u32[]{:S(2)}, u32[]{:S(2)}) collective-permute-start(bf16[8,16,128]{2,1,0:T(8,128)(2,1)S(1)} %get-tuple-element.116), channel_id=1, source_target_pairs={{0,4},{1,5},{2,6},{3,7},{4,0},{5,1},{6,2},{7,3},{8,12},{9,13},{10,... | collective-permute-start | bytes 98312 | tf_op jit(solution)/shard_map/ppermute | solution.py:204
  75.5 1.6 %collective-permute-start.44 = (bf16[8,16,128]{2,1,0:T(8,128)(2,1)S(1)}, bf16[8,16,128]{2,1,0:T(8,128)(2,1)S(1)}, u32[]{:S(2)}, u32[]{:S(2)}) collective-permute-start(bf16[8,16,128]{2,1,0:T(8,128)(2,1)S(1)} %get-tuple-element.118), channel_id=1, source_target_pairs={{0,6},{1,7},{2,4},{3,5},{4,2},{5,3},{6,0},{7,1},{8,14},{9,15},{10,... | collective-permute-start | bytes 98312 | tf_op jit(solution)/shard_map/ppermute | solution.py:204
  77.2 1.7 %collective-permute-start.45 = (bf16[8,16,128]{2,1,0:T(8,128)(2,1)S(1)}, bf16[8,16,128]{2,1,0:T(8,128)(2,1)S(1)}, u32[]{:S(2)}, u32[]{:S(2)}) collective-permute-start(bf16[8,16,128]{2,1,0:T(8,128)(2,1)S(1)} %get-tuple-element.119), channel_id=1, source_target_pairs={{0,7},{1,6},{2,5},{3,4},{4,3},{5,2},{6,1},{7,0},{8,15},{9,14},{10,... | collective-permute-start | bytes 98312 | tf_op jit(solution)/shard_map/ppermute | solution.py:204
  78.8 6.5 %collective-permute-done.43.refs_21_ = bf16[8,16,128]{2,1,0:T(8,128)(2,1)S(1)} collective-permute-done((bf16[8,16,128]{2,1,0:T(8,128)(2,1)S(1)}, bf16[8,16,128]{2,1,0:T(8,128)(2,1)S(1)}, u32[]{:S(2)}, u32[]{:S(2)}) %collective-permute-start.43) | collective-permute-done | bytes 32800 | tf_op jit(solution)/shard_map/ppermute | solution.py:204
  87.9 2.4 %collective-permute-done.47.refs_26_ = bf16[8,16,128]{2,1,0:T(8,128)(2,1)S(1)} collective-permute-done((bf16[8,16,128]{2,1,0:T(8,128)(2,1)S(1)}, bf16[8,16,128]{2,1,0:T(8,128)(2,1)S(1)}, u32[]{:S(2)}, u32[]{:S(2)}) %collective-permute-start.47) | collective-permute-done | bytes 32800 | tf_op jit(solution)/shard_map/ppermute | solution.py:204
  92.5 2.0 %collective-permute-start.16 = (bf16[16,16,128]{2,1,0:T(8,128)(2,1)S(1)}, bf16[16,16,128]{2,1,0:T(8,128)(2,1)S(1)}, u32[]{:S(2)}, u32[]{:S(2)}) collective-permute-start(bf16[16,16,128]{2,1,0:T(8,128)(2,1)S(1)} %get-tuple-element.86), channel_id=1, source_target_pairs={{0,1},{1,0},{2,3},{3,2},{4,5},{5,4},{6,7},{7,6},{8,9},{9,8},{10,11... | collective-permute-start | bytes 196616 | tf_op jit(solution)/shard_map/ppermute | solution.py:204
  98.8 2.2 %collective-permute-done.52.refs_31_ = bf16[8,16,128]{2,1,0:T(8,128)(2,1)S(1)} collective-permute-done((bf16[8,16,128]{2,1,0:T(8,128)(2,1)S(1)}, bf16[8,16,128]{2,1,0:T(8,128)(2,1)S(1)}, u32[]{:S(2)}, u32[]{:S(2)}) %collective-permute-start.52) | collective-permute-done | bytes 32800 | tf_op jit(solution)/shard_map/ppermute | solution.py:204
  110.9 1.5 %collective-permute-start.38 = (bf16[16,16,128]{2,1,0:T(8,128)(2,1)S(1)}, bf16[16,16,128]{2,1,0:T(8,128)(2,1)S(1)}, u32[]{:S(2)}, u32[]{:S(2)}) collective-permute-start(bf16[16,16,128]{2,1,0:T(8,128)(2,1)S(1)} %get-tuple-element.111), channel_id=1, source_target_pairs={{0,7},{1,6},{2,5},{3,4},{4,3},{5,2},{6,1},{7,0},{8,15},{9,14},{10,... | collective-permute-start | bytes 196616 | tf_op jit(solution)/shard_map/ppermute | solution.py:204
  113.5 2.2 %collective-permute-done.37.refs_14_ = bf16[16,16,128]{2,1,0:T(8,128)(2,1)S(1)} collective-permute-done((bf16[16,16,128]{2,1,0:T(8,128)(2,1)S(1)}, bf16[16,16,128]{2,1,0:T(8,128)(2,1)S(1)}, u32[]{:S(2)}, u32[]{:S(2)}) %collective-permute-start.37) | collective-permute-done | bytes 65568 | tf_op jit(solution)/shard_map/ppermute | solution.py:204
  116.5 5.2 %gradient.1 = (f32[8,2,128,128]{3,2,1,0:T(8,128)}, bf16[16,2,128,128]{3,2,1,0:T(8,128)(2,1)}) custom-call(bf16[8,2,128,128]{3,2,1,0:T(8,128)(2,1)S(1)} %copy-done.1, bf16[8,256,256]{2,1,0:T(8,128)(2,1)S(1)} %get-tuple-element.65.source, s32[16]{0:T(128)S(1)} %copy-done.4, bf16[16,16,128]{2,1,0:T(8,128)(2,1)S(1)} %get-tuple-element.85.refs_0_, ...), custom_call_target="tpu_custom_call" | custom-call | bytes 1048576 | tf_op jit(solution)/shard_map/gradient/pallas_call | solution.py:272
  (124 shorter events, 39.4 us)
Async XLA Ops:
  3.9 11.4 %collective-permute-start = (bf16[18,16,128]{2,1,0:T(8,128)(2,1)S(1)}, bf16[18,16,128]{2,1,0:T(8,128)(2,1)S(1)}, u32[]{:S(2)}, u32[]{:S(2)}) collective-permute-start(bf16[18,16,128]{2,1,0:T(8,128)(2,1)S(1)} %get-tuple-element.67), channel_id=1, source_target_pairs={{0,1},{1,0},{2,3},{3,2},{4,5},{5,4},{6,7},{7,6},{8,9},{9,8},{10,11... | collective-permute-start | bytes 221192 | tf_op jit(solution)/shard_map/ppermute | solution.py:204
  4.4 13.7 %collective-permute-start.1 = (bf16[18,16,128]{2,1,0:T(8,128)(2,1)S(1)}, bf16[18,16,128]{2,1,0:T(8,128)(2,1)S(1)}, u32[]{:S(2)}, u32[]{:S(2)}) collective-permute-start(bf16[18,16,128]{2,1,0:T(8,128)(2,1)S(1)} %get-tuple-element.68), channel_id=1, source_target_pairs={{0,2},{1,3},{2,0},{3,1},{4,6},{5,7},{6,4},{7,5},{8,10},{9,11},{10,... | collective-permute-start | bytes 221192 | tf_op jit(solution)/shard_map/ppermute | solution.py:204
  7.0 11.4 %collective-permute-start.2 = (bf16[18,16,128]{2,1,0:T(8,128)(2,1)S(1)}, bf16[18,16,128]{2,1,0:T(8,128)(2,1)S(1)}, u32[]{:S(2)}, u32[]{:S(2)}) collective-permute-start(bf16[18,16,128]{2,1,0:T(8,128)(2,1)S(1)} %get-tuple-element.69), channel_id=1, source_target_pairs={{0,3},{1,2},{2,1},{3,0},{4,7},{5,6},{6,5},{7,4},{8,11},{9,10},{10,... | collective-permute-start | bytes 221192 | tf_op jit(solution)/shard_map/ppermute | solution.py:204
  7.0 11.8 %collective-permute-start.3 = (bf16[18,16,128]{2,1,0:T(8,128)(2,1)S(1)}, bf16[18,16,128]{2,1,0:T(8,128)(2,1)S(1)}, u32[]{:S(2)}, u32[]{:S(2)}) collective-permute-start(bf16[18,16,128]{2,1,0:T(8,128)(2,1)S(1)} %get-tuple-element.70), channel_id=1, source_target_pairs={{0,4},{1,5},{2,6},{3,7},{4,0},{5,1},{6,2},{7,3},{8,12},{9,13},{10,... | collective-permute-start | bytes 221192 | tf_op jit(solution)/shard_map/ppermute | solution.py:204
  8.8 11.8 %collective-permute-start.4 = (bf16[18,16,128]{2,1,0:T(8,128)(2,1)S(1)}, bf16[18,16,128]{2,1,0:T(8,128)(2,1)S(1)}, u32[]{:S(2)}, u32[]{:S(2)}) collective-permute-start(bf16[18,16,128]{2,1,0:T(8,128)(2,1)S(1)} %get-tuple-element.71), channel_id=1, source_target_pairs={{0,5},{1,4},{2,7},{3,6},{4,1},{5,0},{6,3},{7,2},{8,13},{9,12},{10,... | collective-permute-start | bytes 221192 | tf_op jit(solution)/shard_map/ppermute | solution.py:204
  18.8 6.8 %collective-permute-start.8 = (bf16[16,16,128]{2,1,0:T(8,128)(2,1)S(1)}, bf16[16,16,128]{2,1,0:T(8,128)(2,1)S(1)}, u32[]{:S(2)}, u32[]{:S(2)}) collective-permute-start(bf16[16,16,128]{2,1,0:T(8,128)(2,1)S(1)} %get-tuple-element.76), channel_id=1, source_target_pairs={{0,2},{1,3},{2,0},{3,1},{4,6},{5,7},{6,4},{7,5},{8,10},{9,11},{10,... | collective-permute-start | bytes 196616 | tf_op jit(solution)/shard_map/ppermute | solution.py:204
  26.8 6.2 %collective-permute-start.24 = (bf16[16,16,128]{2,1,0:T(8,128)(2,1)S(1)}, bf16[16,16,128]{2,1,0:T(8,128)(2,1)S(1)}, u32[]{:S(2)}, u32[]{:S(2)}) collective-permute-start(bf16[16,16,128]{2,1,0:T(8,128)(2,1)S(1)} %get-tuple-element.95), channel_id=1, source_target_pairs={{0,2},{1,3},{2,0},{3,1},{4,6},{5,7},{6,4},{7,5},{8,10},{9,11},{10,... | collective-permute-start | bytes 196616 | tf_op jit(solution)/shard_map/ppermute | solution.py:204
  28.3 7.5 %collective-permute-start.25 = (bf16[16,16,128]{2,1,0:T(8,128)(2,1)S(1)}, bf16[16,16,128]{2,1,0:T(8,128)(2,1)S(1)}, u32[]{:S(2)}, u32[]{:S(2)}) collective-permute-start(bf16[16,16,128]{2,1,0:T(8,128)(2,1)S(1)} %get-tuple-element.96), channel_id=1, source_target_pairs={{0,3},{1,2},{2,1},{3,0},{4,7},{5,6},{6,5},{7,4},{8,11},{9,10},{10,... | collective-permute-start | bytes 196616 | tf_op jit(solution)/shard_map/ppermute | solution.py:204
  29.8 8.8 %collective-permute-start.26 = (bf16[16,16,128]{2,1,0:T(8,128)(2,1)S(1)}, bf16[16,16,128]{2,1,0:T(8,128)(2,1)S(1)}, u32[]{:S(2)}, u32[]{:S(2)}) collective-permute-start(bf16[16,16,128]{2,1,0:T(8,128)(2,1)S(1)} %get-tuple-element.97), channel_id=1, source_target_pairs={{0,4},{1,5},{2,6},{3,7},{4,0},{5,1},{6,2},{7,3},{8,12},{9,13},{10,... | collective-permute-start | bytes 196616 | tf_op jit(solution)/shard_map/ppermute | solution.py:204
  31.5 7.1 %collective-permute-start.27 = (bf16[16,16,128]{2,1,0:T(8,128)(2,1)S(1)}, bf16[16,16,128]{2,1,0:T(8,128)(2,1)S(1)}, u32[]{:S(2)}, u32[]{:S(2)}) collective-permute-start(bf16[16,16,128]{2,1,0:T(8,128)(2,1)S(1)} %get-tuple-element.98), channel_id=1, source_target_pairs={{0,5},{1,4},{2,7},{3,6},{4,1},{5,0},{6,3},{7,2},{8,13},{9,12},{10,... | collective-permute-start | bytes 196616 | tf_op jit(solution)/shard_map/ppermute | solution.py:204
  32.0 6.6 %collective-permute-start.28 = (bf16[16,16,128]{2,1,0:T(8,128)(2,1)S(1)}, bf16[16,16,128]{2,1,0:T(8,128)(2,1)S(1)}, u32[]{:S(2)}, u32[]{:S(2)}) collective-permute-start(bf16[16,16,128]{2,1,0:T(8,128)(2,1)S(1)} %get-tuple-element.99), channel_id=1, source_target_pairs={{0,6},{1,7},{2,4},{3,5},{4,2},{5,3},{6,0},{7,1},{8,14},{9,15},{10,... | collective-permute-start | bytes 196616 | tf_op jit(solution)/shard_map/ppermute | solution.py:204
  35.9 21.2 %collective-permute-start.14 = (bf16[64,16,128]{2,1,0:T(8,128)(2,1)S(1)}, bf16[64,16,128]{2,1,0:T(8,128)(2,1)S(1)}, u32[]{:S(2)}, u32[]{:S(2)}) collective-permute-start(bf16[64,16,128]{2,1,0:T(8,128)(2,1)S(1)} %get-tuple-element.83), channel_id=1, source_target_pairs={{0,8},{1,9},{2,10},{3,11},{4,12},{5,13},{6,14},{7,15},{8,0},{9,1},... | collective-permute-start | bytes 786440 | tf_op jit(solution)/shard_map/ppermute | solution.py:204
  39.9 28.5 %collective-permute-start.30 = (bf16[64,16,128]{2,1,0:T(8,128)(2,1)S(1)}, bf16[64,16,128]{2,1,0:T(8,128)(2,1)S(1)}, u32[]{:S(2)}, u32[]{:S(2)}) collective-permute-start(bf16[64,16,128]{2,1,0:T(8,128)(2,1)S(1)} %get-tuple-element.102), channel_id=1, source_target_pairs={{0,8},{1,9},{2,10},{3,11},{4,12},{5,13},{6,14},{7,15},{8,0},{9,1},... | collective-permute-start | bytes 786440 | tf_op jit(solution)/shard_map/ppermute | solution.py:204
  57.3 33.1 %collective-permute-start.15 = (bf16[64,16,128]{2,1,0:T(8,128)(2,1)S(1)}, bf16[64,16,128]{2,1,0:T(8,128)(2,1)S(1)}, u32[]{:S(2)}, u32[]{:S(2)}) collective-permute-start(bf16[64,16,128]{2,1,0:T(8,128)(2,1)S(1)} %get-tuple-element.84.refs_0_), channel_id=1, source_target_pairs={{0,8},{1,9},{2,10},{3,11},{4,12},{5,13},{6,14},{7,15},{8,0},{9,1},... | collective-permute-start | bytes 786440 | tf_op jit(solution)/shard_map/ppermute | solution.py:204
  68.5 28.1 %collective-permute-start.31 = (bf16[64,16,128]{2,1,0:T(8,128)(2,1)S(1)}, bf16[64,16,128]{2,1,0:T(8,128)(2,1)S(1)}, u32[]{:S(2)}, u32[]{:S(2)}) collective-permute-start(bf16[64,16,128]{2,1,0:T(8,128)(2,1)S(1)} %get-tuple-element.103.refs_0_), channel_id=1, source_target_pairs={{0,8},{1,9},{2,10},{3,11},{4,12},{5,13},{6,14},{7,15},{8,0},{9,1},... | collective-permute-start | bytes 786440 | tf_op jit(solution)/shard_map/ppermute | solution.py:204
  70.5 6.6 %collective-permute-start.42 = (bf16[8,16,128]{2,1,0:T(8,128)(2,1)S(1)}, bf16[8,16,128]{2,1,0:T(8,128)(2,1)S(1)}, u32[]{:S(2)}, u32[]{:S(2)}) collective-permute-start(bf16[8,16,128]{2,1,0:T(8,128)(2,1)S(1)} %get-tuple-element.116), channel_id=1, source_target_pairs={{0,4},{1,5},{2,6},{3,7},{4,0},{5,1},{6,2},{7,3},{8,12},{9,13},{10,... | collective-permute-start | bytes 98312 | tf_op jit(solution)/shard_map/ppermute | solution.py:204
  74.2 11.1 %collective-permute-start.43 = (bf16[8,16,128]{2,1,0:T(8,128)(2,1)S(1)}, bf16[8,16,128]{2,1,0:T(8,128)(2,1)S(1)}, u32[]{:S(2)}, u32[]{:S(2)}) collective-permute-start(bf16[8,16,128]{2,1,0:T(8,128)(2,1)S(1)} %get-tuple-element.117), channel_id=1, source_target_pairs={{0,5},{1,4},{2,7},{3,6},{4,1},{5,0},{6,3},{7,2},{8,13},{9,12},{10,... | collective-permute-start | bytes 98312 | tf_op jit(solution)/shard_map/ppermute | solution.py:204
  75.5 10.9 %collective-permute-start.44 = (bf16[8,16,128]{2,1,0:T(8,128)(2,1)S(1)}, bf16[8,16,128]{2,1,0:T(8,128)(2,1)S(1)}, u32[]{:S(2)}, u32[]{:S(2)}) collective-permute-start(bf16[8,16,128]{2,1,0:T(8,128)(2,1)S(1)} %get-tuple-element.118), channel_id=1, source_target_pairs={{0,6},{1,7},{2,4},{3,5},{4,2},{5,3},{6,0},{7,1},{8,14},{9,15},{10,... | collective-permute-start | bytes 98312 | tf_op jit(solution)/shard_map/ppermute | solution.py:204
  77.2 10.7 %collective-permute-start.45 = (bf16[8,16,128]{2,1,0:T(8,128)(2,1)S(1)}, bf16[8,16,128]{2,1,0:T(8,128)(2,1)S(1)}, u32[]{:S(2)}, u32[]{:S(2)}) collective-permute-start(bf16[8,16,128]{2,1,0:T(8,128)(2,1)S(1)} %get-tuple-element.119), channel_id=1, source_target_pairs={{0,7},{1,6},{2,5},{3,4},{4,3},{5,2},{6,1},{7,0},{8,15},{9,14},{10,... | collective-permute-start | bytes 98312 | tf_op jit(solution)/shard_map/ppermute | solution.py:204
  87.9 6.6 %collective-permute-start.49 = (bf16[8,16,128]{2,1,0:T(8,128)(2,1)S(1)}, bf16[8,16,128]{2,1,0:T(8,128)(2,1)S(1)}, u32[]{:S(2)}, u32[]{:S(2)}) collective-permute-start(bf16[8,16,128]{2,1,0:T(8,128)(2,1)S(1)} %get-tuple-element.124), channel_id=1, source_target_pairs={{0,4},{1,5},{2,6},{3,7},{4,0},{5,1},{6,2},{7,3},{8,12},{9,13},{10,... | collective-permute-start | bytes 98312 | tf_op jit(solution)/shard_map/ppermute | solution.py:204
  92.5 9.8 %collective-permute-start.16 = (bf16[16,16,128]{2,1,0:T(8,128)(2,1)S(1)}, bf16[16,16,128]{2,1,0:T(8,128)(2,1)S(1)}, u32[]{:S(2)}, u32[]{:S(2)}) collective-permute-start(bf16[16,16,128]{2,1,0:T(8,128)(2,1)S(1)} %get-tuple-element.86), channel_id=1, source_target_pairs={{0,1},{1,0},{2,3},{3,2},{4,5},{5,4},{6,7},{7,6},{8,9},{9,8},{10,11... | collective-permute-start | bytes 196616 | tf_op jit(solution)/shard_map/ppermute | solution.py:204
  94.5 9.2 %collective-permute-start.17 = (bf16[16,16,128]{2,1,0:T(8,128)(2,1)S(1)}, bf16[16,16,128]{2,1,0:T(8,128)(2,1)S(1)}, u32[]{:S(2)}, u32[]{:S(2)}) collective-permute-start(bf16[16,16,128]{2,1,0:T(8,128)(2,1)S(1)} %get-tuple-element.87), channel_id=1, source_target_pairs={{0,2},{1,3},{2,0},{3,1},{4,6},{5,7},{6,4},{7,5},{8,10},{9,11},{10,... | collective-permute-start | bytes 196616 | tf_op jit(solution)/shard_map/ppermute | solution.py:204
  94.8 9.8 %collective-permute-start.18 = (bf16[16,16,128]{2,1,0:T(8,128)(2,1)S(1)}, bf16[16,16,128]{2,1,0:T(8,128)(2,1)S(1)}, u32[]{:S(2)}, u32[]{:S(2)}) collective-permute-start(bf16[16,16,128]{2,1,0:T(8,128)(2,1)S(1)} %get-tuple-element.88), channel_id=1, source_target_pairs={{0,3},{1,2},{2,1},{3,0},{4,7},{5,6},{6,5},{7,4},{8,11},{9,10},{10,... | collective-permute-start | bytes 196616 | tf_op jit(solution)/shard_map/ppermute | solution.py:204
  96.0 9.4 %collective-permute-start.19 = (bf16[16,16,128]{2,1,0:T(8,128)(2,1)S(1)}, bf16[16,16,128]{2,1,0:T(8,128)(2,1)S(1)}, u32[]{:S(2)}, u32[]{:S(2)}) collective-permute-start(bf16[16,16,128]{2,1,0:T(8,128)(2,1)S(1)} %get-tuple-element.89), channel_id=1, source_target_pairs={{0,4},{1,5},{2,6},{3,7},{4,0},{5,1},{6,2},{7,3},{8,12},{9,13},{10,... | collective-permute-start | bytes 196616 | tf_op jit(solution)/shard_map/ppermute | solution.py:204
  (36 other events, 160.3 us)

commit v2 on v0

v2 whole, which is shorter than its diff:
```python
import functools

import jax
import jax.numpy as jnp
from jax import lax
from jax.experimental import pallas as pl
from jax.experimental.pallas import tpu as pltpu
from jax.sharding import PartitionSpec as P

GROUP = 16
BF16 = jnp.bfloat16
F32 = jnp.float32
VMEM = pl.BlockSpec(memory_space=pltpu.VMEM)
SMEM = pl.BlockSpec(memory_space=pltpu.SMEM)
HBM = pl.BlockSpec(memory_space=pltpu.HBM)


def call(kernel, name, out_shape, in_specs, scratch=(), out_specs=None):
    return pl.pallas_call(
        kernel,
        name=name,
        out_shape=out_shape,
        in_specs=in_specs,
        out_specs=out_specs or jax.tree.map(lambda _: VMEM, out_shape),
        scratch_shapes=list(scratch),
        cost_estimate=pl.CostEstimate(flops=0, bytes_accessed=1 << 20, transcendentals=0),
        compiler_params=pltpu.CompilerParams(vmem_limit_bytes=48 * 1024 * 1024),
    )


def pack(real, imag):
    return jnp.concatenate([real, imag], axis=0).astype(BF16)


def parts_kernel(
    data_hbm, wavelet_hbm, panel_hbm, tiles_hbm, rows_hbm, freqs_hbm,
    source, out, data, wavelet, panel, tiles, rows, freqs, sems,
):
    freq_count, _, block, shots = data.shape
    slots = tiles.shape[0]
    height = out.shape[2]
    piece = height // 2
    pairs = (
        (data_hbm, data),
        (tiles_hbm, tiles),
        (wavelet_hbm, wavelet),
        (panel_hbm, panel),
        (freqs_hbm, freqs),
        (rows_hbm, rows),
    )
    copies = [pltpu.make_async_copy(*pair, sems.at[i]) for i, pair in enumerate(pairs)]
    for copy in copies:
        copy.start()
    diagonal = (
        lax.broadcasted_iota(jnp.int32, (block, shots), 0)
        == lax.broadcasted_iota(jnp.int32, (block, shots), 1)
    ).astype(F32)
    for i in (2, 3, 4, 5, 0):
        copies[i].wait()
    identity = diagonal * (lax.axis_index("tiles") == panel[0]).astype(F32)
    lists = slots // height
    for f in range(freq_count):
        real, imag = data[f, 0].astype(F32), data[f, 1].astype(F32)
        source[f, 0] = (wavelet[0, f] * identity - real).astype(BF16)
        source[f, 1] = (wavelet[1, f] * identity - imag).astype(BF16)
        for j in range(GROUP):
            at = slice(j * piece, (j + 1) * piece)
            out[j, slots + lists + f] = pack(real[at], imag[at])
    line = lax.broadcasted_iota(jnp.int32, (height, shots), 0)
    lane = lax.broadcasted_iota(jnp.int32, (height, shots), 1)
    for b in range(lists):
        values = jnp.zeros((height, shots), F32)
        for r in range(height):
            t = b * height + r
            pair = jnp.where(lane < shots // 2, rows[t].astype(F32), freqs[t].astype(F32))
            values = jnp.where(line == r, pair, values)
        for j in range(GROUP):
            out[j, slots + b] = values.astype(BF16)
    copies[1].wait()

    def one(t, carry):
        f = freqs[t]
        left = tiles[t].reshape(2 * block, block)
        right = jnp.concatenate([source[f, 0], source[f, 1]], axis=1)
        product = jnp.dot(left, right, preferred_element_type=F32)
        real = product[:block, :shots] - product[block:, shots:]
        imag = product[:block, shots:] + product[block:, :shots]
        for j in range(GROUP):
            at = slice(j * piece, (j + 1) * piece)
            out[j, t] = pack(real[at], imag[at])
        return carry

    lax.fori_loop(0, slots, one, 0, unroll=4)


def add_parts(freq_count, slots, index, parts, total):
    total[...] = jnp.zeros_like(total)
    for j in range(GROUP):

        def add(t, carry, j=j):
            total[index[j, t]] += parts[j, t].astype(F32)
            return carry

        lax.fori_loop(0, slots, add, 0, unroll=8)


def own_rows(freq_count, slots, got, own, parts, rounded, out):
    first = parts.shape[1] - freq_count
    for j in range(GROUP):
        at = slice(j * freq_count, (j + 1) * freq_count)
        predicted = own[at]
        for ref in got:
            predicted += ref[at].astype(F32)
        rounded[at] = (parts[j, first:].astype(F32) - predicted).astype(BF16)
        out[j, slots:] = predicted.astype(BF16)


def take_rows(slots, index, table, out):
    for j in range(GROUP):

        def take(t, carry, j=j):
            out[j, t] = table[index[j, t]]
            return carry

        lax.fori_loop(0, slots, take, 0, unroll=8)


def whole_kernel(freq_count, slots, index, parts, out, total, table):
    add_parts(freq_count, slots, index, parts, total)
    own_rows(freq_count, slots, (), total, parts, table, out)
    take_rows(slots, index, table, out)


def sum_kernel(freq_count, slots, index, parts, own, *refs):
    sends, total = refs[:-1], refs[-1]
    group = lax.div(lax.axis_index("tiles"), GROUP)
    span = GROUP * freq_count
    add_parts(freq_count, slots, index, parts, total)
    own[...] = total[pl.ds(group * span, span)]
    for q, send in enumerate(sends, 1):
        send[...] = total[pl.ds((group ^ q) * span, span)].astype(BF16)


def residual_kernel(freq_count, slots, own, parts, *refs):
    got, (rounded, back) = refs[:-2], refs[-2:]
    own_rows(freq_count, 0, got, own, parts, rounded, back)


def spread_kernel(freq_count, slots, index, back, *refs):
    have, (out, table) = refs[:-2], refs[-2:]
    group = lax.div(lax.axis_index("tiles"), GROUP)
    span = GROUP * freq_count
    for q, ref in enumerate(have):
        table[pl.ds((group ^ q) * span, span)] = ref[...]
    out[:, slots:] = back[...]
    take_rows(slots, index, table, out)


def gradient_kernel(
    data, source, freqs, arrived, residual_hbm, gradient_hbm, residual, gradient, sems
):
    freq_count, _, block, shots = data.shape
    slots, height = gradient.shape[0], arrived.shape[2]
    piece = height // 2
    scale = 1.0 / shots
    for f in range(freq_count):
        real, imag = data[f, 0].astype(F32), data[f, 1].astype(F32)
        for j in range(GROUP):
            at = slice(j * piece, (j + 1) * piece)
            predicted = arrived[j, slots + f].astype(F32)
            residual[f, 0, at, :] = real[at] - predicted[:piece]
            residual[f, 1, at, :] = imag[at] - predicted[piece:]
    copies = [pltpu.make_async_copy(residual, residual_hbm, sems.at[0])]
    copies[0].start()
    parts = 4
    step = slots // parts

    def one(t, carry):
        left = arrived[:, t].reshape(GROUP * height, shots)
        right = source[freqs[t]].reshape(2 * block, shots)
        total = -scale * lax.dot_general(
            left, right, (((1,), (1,)), ((), ())), preferred_element_type=F32
        )
        real, imag = [], []
        for j in range(GROUP):
            upper = total[j * height : j * height + piece]
            lower = total[j * height + piece : (j + 1) * height]
            real.append(upper[:, :block] + lower[:, block:])
            imag.append(lower[:, :block] - upper[:, block:])
        gradient[t, 0] = jnp.concatenate(real, axis=0).astype(BF16)
        gradient[t, 1] = jnp.concatenate(imag, axis=0).astype(BF16)
        return carry

    for i in range(parts):
        lax.fori_loop(i * step, (i + 1) * step, one, 0, unroll=4)
        at = pl.ds(i * step, step)
        copies.append(
            pltpu.make_async_copy(gradient.at[at], gradient_hbm.at[at], sems.at[i + 1])
        )
        copies[-1].start()
    for copy in copies:
        copy.wait()


def per_device(data, wavelet, panel_block, tiles, cover_rows, cover_freqs):
    freq_count, _, block, shots = data.shape
    slots = tiles.shape[0]
    peers = lax.axis_size("tiles")
    groups = peers // GROUP
    height = 2 * block // GROUP
    span = GROUP * freq_count
    sizes = (freq_count, slots)
    members = [list(range(g * GROUP, (g + 1) * GROUP)) for g in range(groups)]

    def shape(count, kind=BF16):
        return jax.ShapeDtypeStruct((count, height, shots), kind)

    def payload(count):
        return jax.ShapeDtypeStruct((GROUP, count, height, shots), BF16)

    def exchange(value):
        return lax.all_to_all(
            value, "tiles", split_axis=0, concat_axis=0, tiled=True, axis_index_groups=members
        )

    def across(values):
        return [
            lax.ppermute(value, "tiles", [(i, i ^ (q * GROUP)) for i in range(peers)])
            for q, value in enumerate(values, 1)
        ]

    source, sent = call(
        parts_kernel,
        "parts",
        [
            jax.ShapeDtypeStruct(data.shape, BF16),
            payload(slots + slots // height + freq_count),
        ],
        [HBM] * 6,
        scratch=[
            pltpu.VMEM(data.shape, BF16),
            pltpu.SMEM((2, freq_count), F32),
            pltpu.SMEM((1,), jnp.int32),
            pltpu.VMEM(tiles.shape, BF16),
            pltpu.SMEM((slots,), jnp.int32),
            pltpu.SMEM((slots,), jnp.int32),
            pltpu.SemaphoreType.DMA((6,)),
        ],
    )(data, wavelet.T, panel_block, tiles, cover_rows, cover_freqs)
    parts = exchange(sent)
    lists = parts[:, slots:-freq_count].reshape(GROUP, slots, shots).astype(jnp.int32)
    index = lists[:, :, 0] * freq_count + lists[:, :, shots // 2]
    total = pltpu.VMEM((peers * freq_count, height, shots), F32)
    table = pltpu.VMEM((peers * freq_count, height, shots), BF16)
    if groups == 1:
        returns = call(
            functools.partial(whole_kernel, *sizes),
            "residual_slices",
            payload(slots + freq_count),
            [SMEM, VMEM],
            scratch=[total, table],
        )(index, parts)
    else:
        own, *sends = call(
            functools.partial(sum_kernel, *sizes),
            "sums",
            [shape(span, F32)] + [shape(span)] * (groups - 1),
            [SMEM, VMEM],
            scratch=[total],
        )(index, parts)
        mine, back = call(
            functools.partial(residual_kernel, *sizes),
            "residual_slices",
            [shape(span), payload(freq_count)],
            [VMEM] * (1 + groups),
        )(own, parts, *across(sends))
        returns = call(
            functools.partial(spread_kernel, *sizes),
            "spread",
            payload(slots + freq_count),
            [SMEM] + [VMEM] * (1 + groups),
            scratch=[table],
        )(index, back, mine, *across([mine] * (groups - 1)))
    return call(
        gradient_kernel,
        "gradient",
        (jax.ShapeDtypeStruct(data.shape, F32), jax.ShapeDtypeStruct(tiles.shape, BF16)),
        [VMEM, VMEM, SMEM, VMEM],
        out_specs=(HBM, HBM),
        scratch=[
            pltpu.VMEM(data.shape, F32),
            pltpu.VMEM(tiles.shape, BF16),
            pltpu.SemaphoreType.DMA((5,)),
        ],
    )(data, source, cover_freqs, exchange(returns))


def solution(mesh):
    in_specs = (
        P("windows", None, "tiles", None),
        P(),
        P(),
        P(("windows", "tiles"), None, None, None),
        P(("windows", "tiles")),
        P(("windows", "tiles")),
    )
    out_specs = (P("windows", None, "tiles", None), P(("windows", "tiles"), None, None, None))
    return jax.shard_map(
        per_device, mesh=mesh, in_specs=in_specs, out_specs=out_specs, check_vma=False
    )
```

time: 139 us -> 99.7 us (0.72)
  the two profiles are of different devices: /device:TPU:15 before, /device:TPU:0 now
where the time goes in v2:
time: 99.7 us; the launch traced here: 99 us
  blocking collectives  86 us (86%)
  Pallas kernels  6.98 us (7%)
  local copies, waits for them, and re-layouts  4.26 us (4%)
  between operations  1.33 us (1%)
    all_to_all x2, blocking collectives, exchange(): lax.all_to_all(value, 'tiles', split_axis=0, concat_axis=0, tiled=True, a...  86 us
    unnamed x14, local copies, waits for them, and re-layouts  4.26 us
    pallas_call x1, Pallas kernels, per_device(): call(functools.partial(whole_kernel, *sizes), 'residual_slices', payload(...  2.61 us
    pallas_call x1, Pallas kernels, per_device(): call(gradient_kernel, 'gradient', (jax.ShapeDtypeStruct(data.shape, F32),...  2.28 us
    pallas_call x1, Pallas kernels, per_device(): call(parts_kernel, 'parts', [jax.ShapeDtypeStruct(data.shape, BF16), payl...  2.08 us

profile of v2, /device:TPU:0, one launch (start us, length us, event | category | flops | bytes accessed | tf_op | source)
XLA Modules:
  0.0 99.0 jit_solution(10582796765959026649)
XLA Ops:
  1.3 0.0 copy-start
  1.3 1.0 %copy-done = bf16[8,2,128,128]{3,2,1,0:T(8,128)(2,1)S(1)} copy-done((bf16[8,2,128,128]{3,2,1,0:T(8,128)(2,1)S(1)}, bf16[8,2,128,128]{3,2,1,0:T(8,128)(2,1)}, u32[]{:S(2)}) %copy-start) | copy-done | bytes 524312
  2.3 0.0 copy-start.2
  2.3 1.2 %copy-done.2 = bf16[16,2,128,128]{3,2,1,0:T(8,128)(2,1)S(1)} copy-done((bf16[16,2,128,128]{3,2,1,0:T(8,128)(2,1)S(1)}, bf16[16,2,128,128]{3,2,1,0:T(8,128)(2,1)}, u32[]{:S(2)}) %copy-start.2) | copy-done | bytes 1048600
  3.5 0.0 copy-start.3
  3.5 0.7 copy-done.3
  4.2 0.0 copy-start.5
  4.2 0.7 copy-done.5
  4.9 0.0 copy-start.6
  4.9 0.7 copy-done.6
  5.5 2.1 %parts.1 = (bf16[8,2,128,128]{3,2,1,0:T(8,128)(2,1)S(1)}, bf16[16,25,16,128]{3,2,1,0:T(8,128)(2,1)S(1)}) custom-call(bf16[8,2,128,128]{3,2,1,0:T(8,128)(2,1)S(1)} %copy-done, f32[2,8]{1,0:T(2,128)S(1)} %bitcast.6, s32[1]{0:T(128)S(6)} %copy.8.panel_hbm, bf16[16,2,128,128]{3,2,1,0:T(8,128)(2,1)S(1)} %copy-done.2, s32[16]{0:T(128)S(1)} %copy-done.6, ...), custom_call_target="tpu_custom_call" | custom-call | bytes 1048576 | tf_op jit(solution)/shard_map/parts/pallas_call | solution.py:232
  7.6 46.9 %all_to_all.10.parts = bf16[16,25,16,128]{3,2,1,0:T(8,128)(2,1)S(1)} all-to-all(bf16[16,25,16,128]{3,2,1,0:T(8,128)(2,1)S(1)} %get-tuple-element.5), channel_id=1, replica_groups={{0,1,2,3,4,5,6,7,8,9,10,11,12,13,14,15},{16,17,18,19,20,21,22,23,24,25,..., dimensions={0} | all-to-all | bytes 3276800 | tf_op jit(solution)/shard_map/all_to_all | solution.py:222
  54.6 0.4 fusion.index
  55.0 2.6 %residual_slices.1 = bf16[16,24,16,128]{3,2,1,0:T(8,128)(2,1)S(1)} custom-call(s32[16,16]{1,0:T(8,128)S(1)} %fusion.index, bf16[16,25,16,128]{3,2,1,0:T(8,128)(2,1)S(1)} %all_to_all.10.parts), custom_call_target="tpu_custom_call" | custom-call | bytes 1048576 | tf_op jit(solution)/shard_map/residual_slices/pallas_call | solution.py:256
  57.6 0.0 copy-start.1
  57.7 0.0 copy-start.4
  57.7 39.1 %all_to_all.11.arrived = bf16[16,24,16,128]{3,2,1,0:T(8,128)(2,1)S(1)} all-to-all(bf16[16,24,16,128]{3,2,1,0:T(8,128)(2,1)S(1)} %residual_slices.1), channel_id=1, replica_groups={{0,1,2,3,4,5,6,7,8,9,10,11,12,13,14,15},{16,17,18,19,20,21,22,23,24,25,..., dimensions={0} | all-to-all | bytes 3145728 | tf_op jit(solution)/shard_map/all_to_all | solution.py:222
  96.7 0.0 copy-done.1
  96.7 0.0 copy-done.4
  96.7 2.3 %gradient.1 = (f32[8,2,128,128]{3,2,1,0:T(8,128)}, bf16[16,2,128,128]{3,2,1,0:T(8,128)(2,1)}) custom-call(bf16[8,2,128,128]{3,2,1,0:T(8,128)(2,1)S(1)} %copy-done.1, bf16[8,2,128,128]{3,2,1,0:T(8,128)(2,1)S(1)} %get-tuple-element.4.source, s32[16]{0:T(128)S(1)} %copy-done.4, bf16[16,24,16,128]{3,2,1,0:T(8,128)(2,1)S(1)} %all_to_all.11.arrived), custom_call_target="tpu_custom_call" | custom-call | bytes 1048576 | tf_op jit(solution)/shard_map/gradient/pallas_call | solution.py:284
  (1 shorter events, 0.0 us)
Async XLA Ops:
  1.3 1.0 %copy-start = (bf16[8,2,128,128]{3,2,1,0:T(8,128)(2,1)S(1)}, bf16[8,2,128,128]{3,2,1,0:T(8,128)(2,1)}, u32[]{:S(2)}) copy-start(bf16[8,2,128,128]{3,2,1,0:T(8,128)(2,1)} %data.1) | copy-start | bytes 1572868
  2.3 1.2 %copy-start.2 = (bf16[16,2,128,128]{3,2,1,0:T(8,128)(2,1)S(1)}, bf16[16,2,128,128]{3,2,1,0:T(8,128)(2,1)}, u32[]{:S(2)}) copy-start(bf16[16,2,128,128]{3,2,1,0:T(8,128)(2,1)} %tiles_hbm.1) | copy-start | bytes 3145732
  3.5 0.7 copy-start.3
  4.2 0.7 copy-start.5
  4.9 0.7 copy-start.6
  57.6 39.1 %copy-start.1 = (bf16[8,2,128,128]{3,2,1,0:T(8,128)(2,1)S(1)}, bf16[8,2,128,128]{3,2,1,0:T(8,128)(2,1)}, u32[]{:S(2)}) copy-start(bf16[8,2,128,128]{3,2,1,0:T(8,128)(2,1)} %data.1) | copy-start | bytes 1572868
  57.7 39.1 %copy-start.4 = (s32[16]{0:T(128)S(1)}, s32[16]{0:T(128)}, u32[]{:S(2)}) copy-start(s32[16]{0:T(128)} %freqs.1) | copy-start | bytes 196

commit v3 on v2

--- a/solution.py
+++ b/solution.py
@@ -15,7 +15,7 @@
 HBM = pl.BlockSpec(memory_space=pltpu.HBM)
 
 
-def call(kernel, name, out_shape, in_specs, scratch=(), out_specs=None):
+def call(kernel, name, out_shape, in_specs, scratch=(), out_specs=None, mib=48):
     return pl.pallas_call(
         kernel,
         name=name,
@@ -24,7 +24,7 @@
         out_specs=out_specs or jax.tree.map(lambda _: VMEM, out_shape),
         scratch_shapes=list(scratch),
         cost_estimate=pl.CostEstimate(flops=0, bytes_accessed=1 << 20, transcendentals=0),
-        compiler_params=pltpu.CompilerParams(vmem_limit_bytes=48 * 1024 * 1024),
+        compiler_params=pltpu.CompilerParams(vmem_limit_bytes=mib * 1024 * 1024),
     )
 
 
@@ -246,6 +246,7 @@
             pltpu.SMEM((slots,), jnp.int32),
             pltpu.SemaphoreType.DMA((6,)),
         ],
+        mib=60,
     )(data, wavelet.T, panel_block, tiles, cover_rows, cover_freqs)
     parts = exchange(sent)
     lists = parts[:, slots:-freq_count].reshape(GROUP, slots, shots).astype(jnp.int32)

time: 99.7 us -> 97.3 us (0.976)
  local copies, waits for them, and re-layouts: 4.26 us -> 0.02 us
  Pallas kernels: 6.98 us -> 8.69 us
    unnamed x14 -> x6, local copies, waits for them, and re-layouts: 4.26 us -> 0.02 us
    pallas_call x1, Pallas kernels: 2.08 us -> 3.79 us  [per_device(): call(parts_kernel, 'parts', [jax.ShapeDtypeStruct(data.shape, BF16), payl...]
where the time goes in v3:
time: 97.3 us; the launch traced here: 96.7 us
  blocking collectives  86.2 us (89%)
  Pallas kernels  8.69 us (9%)
  between operations  1.33 us (1%)
    all_to_all x2, blocking collectives, exchange(): lax.all_to_all(value, 'tiles', split_axis=0, concat_axis=0, tiled=True, a...  86.2 us
    pallas_call x1, Pallas kernels, per_device(): call(parts_kernel, 'parts', [jax.ShapeDtypeStruct(data.shape, BF16), payl...  3.79 us
    pallas_call x1, Pallas kernels, per_device(): call(functools.partial(whole_kernel, *sizes), 'residual_slices', payload(...  2.61 us
    pallas_call x1, Pallas kernels, per_device(): call(gradient_kernel, 'gradient', (jax.ShapeDtypeStruct(data.shape, F32),...  2.29 us

profile of v3, /device:TPU:0, one launch (start us, length us, event | category | flops | bytes accessed | tf_op | source)
XLA Modules:
  0.0 96.7 jit_solution(8911772872481608645)
XLA Ops:
  1.3 3.8 %parts.1 = (bf16[8,2,128,128]{3,2,1,0:T(8,128)(2,1)}, bf16[16,25,16,128]{3,2,1,0:T(8,128)(2,1)}) custom-call(bf16[8,2,128,128]{3,2,1,0:T(8,128)(2,1)} %data.1, f32[2,8]{1,0:T(2,128)} %bitcast.6, s32[1]{0:T(128)S(6)} %copy.8.panel_hbm, bf16[16,2,128,128]{3,2,1,0:T(8,128)(2,1)} %tiles_hbm.1, s32[16]{0:T(128)} %rows_hbm.1, s32[16]{0:T(128)} %freqs.1), custom_call_target="tpu_custom_call" | custom-call | bytes 1048576 | tf_op jit(solution)/shard_map/parts/pallas_call | solution.py:232
  5.1 47.2 %all_to_all.10.parts = bf16[16,25,16,128]{3,2,1,0:T(8,128)(2,1)S(1)} all-to-all(bf16[16,25,16,128]{3,2,1,0:T(8,128)(2,1)} %get-tuple-element.5), channel_id=1, replica_groups={{0,1,2,3,4,5,6,7,8,9,10,11,12,13,14,15},{16,17,18,19,20,21,22,23,24,25,..., dimensions={0} | all-to-all | bytes 3276800 | tf_op jit(solution)/shard_map/all_to_all | solution.py:222
  52.2 0.4 fusion.index
  52.7 2.6 %residual_slices.1 = bf16[16,24,16,128]{3,2,1,0:T(8,128)(2,1)S(1)} custom-call(s32[16,16]{1,0:T(8,128)S(1)} %fusion.index, bf16[16,25,16,128]{3,2,1,0:T(8,128)(2,1)S(1)} %all_to_all.10.parts), custom_call_target="tpu_custom_call" | custom-call | bytes 1048576 | tf_op jit(solution)/shard_map/residual_slices/pallas_call | solution.py:257
  55.3 0.0 copy-start
  55.3 0.0 copy-start.1
  55.3 0.0 copy-start.2
  55.3 39.1 %all_to_all.11.arrived = bf16[16,24,16,128]{3,2,1,0:T(8,128)(2,1)S(1)} all-to-all(bf16[16,24,16,128]{3,2,1,0:T(8,128)(2,1)S(1)} %residual_slices.1), channel_id=1, replica_groups={{0,1,2,3,4,5,6,7,8,9,10,11,12,13,14,15},{16,17,18,19,20,21,22,23,24,25,..., dimensions={0} | all-to-all | bytes 3145728 | tf_op jit(solution)/shard_map/all_to_all | solution.py:222
  94.4 0.0 copy-done
  94.4 0.0 copy-done.1
  94.4 0.0 copy-done.2
  94.4 2.3 %gradient.1 = (f32[8,2,128,128]{3,2,1,0:T(8,128)}, bf16[16,2,128,128]{3,2,1,0:T(8,128)(2,1)}) custom-call(bf16[8,2,128,128]{3,2,1,0:T(8,128)(2,1)S(1)} %copy-done, bf16[8,2,128,128]{3,2,1,0:T(8,128)(2,1)S(1)} %copy-done.1, s32[16]{0:T(128)S(1)} %copy-done.2, bf16[16,24,16,128]{3,2,1,0:T(8,128)(2,1)S(1)} %all_to_all.11.arrived), custom_call_target="tpu_custom_call" | custom-call | bytes 1048576 | tf_op jit(solution)/shard_map/gradient/pallas_call | solution.py:285
  (1 shorter events, 0.0 us)
Async XLA Ops:
  55.3 39.1 %copy-start = (bf16[8,2,128,128]{3,2,1,0:T(8,128)(2,1)S(1)}, bf16[8,2,128,128]{3,2,1,0:T(8,128)(2,1)}, u32[]{:S(2)}) copy-start(bf16[8,2,128,128]{3,2,1,0:T(8,128)(2,1)} %data.1) | copy-start | bytes 1572868
  55.3 39.1 %copy-start.1 = (bf16[8,2,128,128]{3,2,1,0:T(8,128)(2,1)S(1)}, bf16[8,2,128,128]{3,2,1,0:T(8,128)(2,1)}, u32[]{:S(2)}) copy-start(bf16[8,2,128,128]{3,2,1,0:T(8,128)(2,1)} %get-tuple-element.4.source) | copy-start | bytes 1572868
  55.3 39.1 %copy-start.2 = (s32[16]{0:T(128)S(1)}, s32[16]{0:T(128)}, u32[]{:S(2)}) copy-start(s32[16]{0:T(128)} %freqs.1) | copy-start | bytes 196

commit v4 on v3

v4 whole, which is shorter than its diff:
```python
import functools

import jax
import jax.numpy as jnp
from jax import lax
from jax.experimental import pallas as pl
from jax.experimental.pallas import tpu as pltpu
from jax.sharding import PartitionSpec as P

GROUP = 16
BF16 = jnp.bfloat16
F32 = jnp.float32
VMEM = pl.BlockSpec(memory_space=pltpu.VMEM)
SMEM = pl.BlockSpec(memory_space=pltpu.SMEM)
HBM = pl.BlockSpec(memory_space=pltpu.HBM)


def call(kernel, name, out_shape, in_specs, scratch=(), out_specs=None, mib=48):
    return pl.pallas_call(
        kernel,
        name=name,
        out_shape=out_shape,
        in_specs=in_specs,
        out_specs=out_specs or jax.tree.map(lambda _: VMEM, out_shape),
        scratch_shapes=list(scratch),
        cost_estimate=pl.CostEstimate(flops=0, bytes_accessed=1 << 20, transcendentals=0),
        compiler_params=pltpu.CompilerParams(vmem_limit_bytes=mib * 1024 * 1024),
    )


def put(buffer, slot, count, real, imag):
    piece = real.shape[0] // GROUP
    for j in range(GROUP):
        at = slice(j * piece, (j + 1) * piece)
        first = 2 * j * piece * count + slot
        buffer[pl.ds(first, piece, stride=count), :] = real[at]
        buffer[pl.ds(first + piece * count, piece, stride=count), :] = imag[at]


def get(buffer, slot, count, piece, j):
    first = 2 * j * piece * count + slot
    return (
        buffer[pl.ds(first, piece, stride=count), :],
        buffer[pl.ds(first + piece * count, piece, stride=count), :],
    )


def parts_kernel(
    data_hbm, wavelet_hbm, panel_hbm, tiles_hbm, rows_hbm, freqs_hbm,
    source, out, data, wavelet, panel, tiles, rows, freqs, sems, wide, wide_data,
):
    freq_count, _, block, shots = data.shape
    slots = tiles.shape[0]
    height = 2 * block // GROUP
    peers = lax.axis_size("tiles")
    pairs = (
        (data_hbm, data),
        (tiles_hbm, tiles),
        (wavelet_hbm, wavelet),
        (panel_hbm, panel),
        (freqs_hbm, freqs),
        (rows_hbm, rows),
    )
    copies = [pltpu.make_async_copy(*pair, sems.at[i]) for i, pair in enumerate(pairs)]
    for copy in copies:
        copy.start()
    diagonal = (
        lax.broadcasted_iota(jnp.int32, (block, shots), 0)
        == lax.broadcasted_iota(jnp.int32, (block, shots), 1)
    ).astype(F32)
    for i in (2, 3, 4, 5, 0):
        copies[i].wait()
    identity = diagonal * (lax.axis_index("tiles") == panel[0]).astype(F32)
    for f in range(freq_count):
        real, imag = data[f, 0].astype(F32), data[f, 1].astype(F32)
        source[f, 0] = (wavelet[0, f] * identity - real).astype(BF16)
        source[f, 1] = (wavelet[1, f] * identity - imag).astype(BF16)
        put(wide_data, f, freq_count, real, imag)
    line = lax.broadcasted_iota(jnp.int32, (slots, shots), 0)
    targets = jnp.zeros((slots, shots), jnp.int32)
    for t in range(slots):
        targets = jnp.where(line == t, rows[t] * freq_count + freqs[t], targets)
    targets = (targets - peers * freq_count // 2).astype(F32).astype(BF16)
    first, second = height * slots, height * (slots + freq_count)
    for j in range(GROUP):
        at = slice(j * height * freq_count, (j + 1) * height * freq_count)
        out[j, first:second] = wide_data[at].astype(BF16)
        out[j, second:] = targets
    copies[1].wait()

    def one(t, carry):
        f = freqs[t]
        left = tiles[t].reshape(2 * block, block)
        right = jnp.concatenate([source[f, 0], source[f, 1]], axis=1)
        product = jnp.dot(left, right, preferred_element_type=F32)
        real = product[:block, :shots] - product[block:, shots:]
        put(wide, t, slots, real, product[:block, shots:] + product[block:, :shots])
        return carry

    lax.fori_loop(0, slots, one, 0, unroll=4)
    for j in range(GROUP):
        out[j, :first] = wide[j * first : (j + 1) * first].astype(BF16)


def one_hot(slots, peers, freq_count, parts):
    first = parts.shape[1] - slots
    shots = parts.shape[2]
    targets = parts[:, first:].astype(F32).reshape(GROUP * slots, shots)
    count = peers * freq_count
    lane = lax.broadcasted_iota(jnp.int32, (GROUP * slots, shots), 1).astype(F32)
    hot = [
        (targets == lane + float(start - count // 2)).astype(F32).astype(BF16)
        for start in range(0, count, shots)
    ]
    return jnp.concatenate(hot, axis=1) if len(hot) > 1 else hot[0]


def row_of_slots(slots, r, parts):
    at = slice(r * slots, (r + 1) * slots)
    return parts[:, at].reshape(GROUP * slots, parts.shape[2])


def sum_row(hot, row):
    return lax.dot_general(hot, row, (((0,), (0,)), ((), ())), preferred_element_type=F32)


def row_of_data(freq_count, slots, r, height, parts):
    first = height * slots + r * freq_count
    rows = parts[:, first : first + freq_count].astype(F32)
    return rows.reshape(GROUP * freq_count, parts.shape[2])


def put_back(freq_count, first, predicted, out):
    for r in range(0, len(predicted), 2):
        for j in range(GROUP):
            at = slice(j * freq_count, (j + 1) * freq_count)
            rows = jnp.concatenate([predicted[r][at], predicted[r + 1][at]], axis=0)
            out[j, first + r * freq_count : first + (r + 2) * freq_count] = rows.astype(BF16)


def whole_kernel(sizes, parts, out):
    freq_count, slots, peers = sizes
    height = (parts.shape[1] - slots) // (slots + freq_count)
    shots = parts.shape[2]
    hot = one_hot(slots, peers, freq_count, parts)
    step = 2
    for r in range(0, height, step):
        rows = [row_of_slots(slots, r + i, parts) for i in range(step)]
        total = sum_row(hot, jnp.concatenate(rows, axis=1))
        predicted = [total[:, i * shots : (i + 1) * shots] for i in range(step)]
        data = [row_of_data(freq_count, slots, r + i, height, parts) for i in range(step)]
        rounded = jnp.concatenate(
            [(d - p).astype(BF16) for d, p in zip(data, predicted)], axis=1
        )
        picked = jnp.dot(hot, rounded, preferred_element_type=F32).astype(BF16)
        for i in range(step):
            at = slice((r + i) * slots, (r + i + 1) * slots)
            out[:, at] = picked[:, i * shots : (i + 1) * shots].reshape(GROUP, slots, shots)
        put_back(freq_count, height * slots + r * freq_count, predicted, out)


def sum_kernel(sizes, parts, own, *refs):
    freq_count, slots, peers = sizes
    sends, total = refs[:-1], refs[-1]
    span = GROUP * freq_count
    group = lax.div(lax.axis_index("tiles"), GROUP)
    hot = one_hot(slots, peers, freq_count, parts)
    for r in range(own.shape[0]):
        total[...] = sum_row(hot, row_of_slots(slots, r, parts))
        own[r] = total[pl.ds(pl.multiple_of(group * span, span), span)]
        for q, send in enumerate(sends, 1):
            there = pl.multiple_of((group ^ q) * span, span)
            send[r] = total[pl.ds(there, span)].astype(BF16)


def residual_kernel(sizes, own, parts, *refs):
    freq_count, slots, _ = sizes
    got, (rounded, back) = refs[:-2], refs[-2:]
    height = own.shape[0]
    for r in range(0, height, 2):
        predicted = []
        for i in (r, r + 1):
            values = own[i]
            for ref in got:
                values += ref[i].astype(F32)
            predicted.append(values)
            data = row_of_data(freq_count, slots, i, height, parts)
            rounded[i] = (data - values).astype(BF16)
        put_back(freq_count, r * freq_count, predicted, back)


def spread_kernel(sizes, parts, back, *refs):
    freq_count, slots, peers = sizes
    have, (out, table) = refs[:-2], refs[-2:]
    height, span, shots = have[0].shape
    group = lax.div(lax.axis_index("tiles"), GROUP)
    hot = one_hot(slots, peers, freq_count, parts)
    for r in range(height):
        for q, ref in enumerate(have):
            table[pl.ds(pl.multiple_of((group ^ q) * span, span), span)] = ref[r]
        picked = jnp.dot(hot, table[...], preferred_element_type=F32).astype(BF16)
        out[:, r * slots : (r + 1) * slots] = picked.reshape(GROUP, slots, shots)
    out[:, height * slots :] = back[...]


def gradient_kernel(
    data, source, freqs, arrived, residual_hbm, gradient_hbm, residual, gradient, sems, wide, wide_data
):
    freq_count, _, block, shots = data.shape
    slots = gradient.shape[0]
    piece = block // GROUP
    height = 2 * piece
    first = height * slots
    second = first + height * freq_count
    scale = 1.0 / shots
    for j in range(GROUP):
        at = slice(j * height * freq_count, (j + 1) * height * freq_count)
        wide_data[at] = arrived[j, first:second].astype(F32)
    for f in range(freq_count):
        real, imag = data[f, 0].astype(F32), data[f, 1].astype(F32)
        for j in range(GROUP):
            at = slice(j * piece, (j + 1) * piece)
            predicted = get(wide_data, f, freq_count, piece, j)
            residual[f, 0, at, :] = real[at] - predicted[0]
            residual[f, 1, at, :] = imag[at] - predicted[1]
    copies = [pltpu.make_async_copy(residual, residual_hbm, sems.at[0])]
    copies[0].start()
    for j in range(GROUP):
        wide[j * first : (j + 1) * first] = arrived[j, :first].astype(F32)
    parts = 4
    step = slots // parts

    def one(t, carry):
        left = wide[pl.ds(t, GROUP * height, stride=slots), :].astype(BF16)
        right = source[freqs[t]].reshape(2 * block, shots)
        total = -scale * lax.dot_general(
            left, right, (((1,), (1,)), ((), ())), preferred_element_type=F32
        )
        real, imag = [], []
        for j in range(GROUP):
            upper = total[j * height : j * height + piece]
            lower = total[j * height + piece : (j + 1) * height]
            real.append(upper[:, :block] + lower[:, block:])
            imag.append(lower[:, :block] - upper[:, block:])
        gradient[t, 0] = jnp.concatenate(real, axis=0).astype(BF16)
        gradient[t, 1] = jnp.concatenate(imag, axis=0).astype(BF16)
        return carry

    for i in range(parts):
        lax.fori_loop(i * step, (i + 1) * step, one, 0, unroll=4)
        at = pl.ds(i * step, step)
        copies.append(
            pltpu.make_async_copy(gradient.at[at], gradient_hbm.at[at], sems.at[i + 1])
        )
        copies[-1].start()
    for copy in copies:
        copy.wait()


def per_device(data, wavelet, panel_block, tiles, cover_rows, cover_freqs):
    freq_count, _, block, shots = data.shape
    slots = tiles.shape[0]
    peers = lax.axis_size("tiles")
    groups = peers // GROUP
    height = 2 * block // GROUP
    span = GROUP * freq_count
    sizes = (freq_count, slots, peers)
    members = [list(range(g * GROUP, (g + 1) * GROUP)) for g in range(groups)]
    wide = pltpu.VMEM((GROUP * height * slots, shots), F32)
    wide_data = pltpu.VMEM((GROUP * height * freq_count, shots), F32)

    def shape(kind=BF16):
        return jax.ShapeDtypeStruct((height, span, shots), kind)

    def payload(count):
        return jax.ShapeDtypeStruct((GROUP, count, shots), BF16)

    def exchange(value):
        return lax.all_to_all(
            value, "tiles", split_axis=0, concat_axis=0, tiled=True, axis_index_groups=members
        )

    def across(values):
        return [
            lax.ppermute(value, "tiles", [(i, i ^ (q * GROUP)) for i in range(peers)])
            for q, value in enumerate(values, 1)
        ]

    source, sent = call(
        parts_kernel,
        "parts",
        [
            jax.ShapeDtypeStruct(data.shape, BF16),
            payload(height * (slots + freq_count) + slots),
        ],
        [HBM] * 6,
        scratch=[
            pltpu.VMEM(data.shape, BF16),
            pltpu.SMEM((2, freq_count), F32),
            pltpu.SMEM((1,), jnp.int32),
            pltpu.VMEM(tiles.shape, BF16),
            pltpu.SMEM((slots,), jnp.int32),
            pltpu.SMEM((slots,), jnp.int32),
            pltpu.SemaphoreType.DMA((6,)),
            wide,
            wide_data,
        ],
        mib=60,
    )(data, wavelet.T, panel_block, tiles, cover_rows, cover_freqs)
    parts = exchange(sent)
    returns = payload(height * (slots + freq_count))
    if groups == 1:
        out = call(
            functools.partial(whole_kernel, sizes), "residual_slices", returns, [VMEM]
        )(parts)
    else:
        own, *sends = call(
            functools.partial(sum_kernel, sizes),
            "sums",
            [shape(F32)] + [shape()] * (groups - 1),
            [VMEM],
            scratch=[pltpu.VMEM((peers * freq_count, shots), F32)],
        )(parts)
        mine, back = call(
            functools.partial(residual_kernel, sizes),
            "residual_slices",
            [shape(), payload(height * freq_count)],
            [VMEM] * (1 + groups),
        )(own, parts, *across(sends))
        out = call(
            functools.partial(spread_kernel, sizes),
            "spread",
            returns,
            [VMEM] * (2 + groups),
            scratch=[pltpu.VMEM((peers * freq_count, shots), BF16)],
        )(parts, back, mine, *across([mine] * (groups - 1)))
    return call(
        gradient_kernel,
        "gradient",
        (jax.ShapeDtypeStruct(data.shape, F32), jax.ShapeDtypeStruct(tiles.shape, BF16)),
        [VMEM, VMEM, SMEM, VMEM],
        out_specs=(HBM, HBM),
        scratch=[
            pltpu.VMEM(data.shape, F32),
            pltpu.VMEM(tiles.shape, BF16),
            pltpu.SemaphoreType.DMA((5,)),
            wide,
            wide_data,
        ],
    )(data, source, cover_freqs, exchange(out))


def solution(mesh):
    in_specs = (
        P("windows", None, "tiles", None),
        P(),
        P(),
        P(("windows", "tiles"), None, None, None),
        P(("windows", "tiles")),
        P(("windows", "tiles")),
    )
    out_specs = (P("windows", None, "tiles", None), P(("windows", "tiles"), None, None, None))
    return jax.shard_map(
        per_device, mesh=mesh, in_specs=in_specs, out_specs=out_specs, check_vma=False
    )
```

time: 97.3 us -> 96.5 us (level)
    pallas_call x1, Pallas kernels: 2.61 us -> 1.14 us  [per_device(): call(functools.partial(whole_kernel, sizes), 'residual_slices', returns,...]
where the time goes in v4:
time: 96.5 us; the launch traced here: 95.9 us
  blocking collectives  86.2 us (89%)
  Pallas kernels  8.32 us (9%)
  between operations  1.32 us (1%)
    all_to_all x2, blocking collectives, exchange(): lax.all_to_all(value, 'tiles', split_axis=0, concat_axis=0, tiled=True, a...  86.2 us
    pallas_call x1, Pallas kernels, per_device(): call(parts_kernel, 'parts', [jax.ShapeDtypeStruct(data.shape, BF16), payl...  4.47 us
    pallas_call x1, Pallas kernels, per_device(): call(gradient_kernel, 'gradient', (jax.ShapeDtypeStruct(data.shape, F32),...  2.71 us

profile of v4, /device:TPU:0, one launch (start us, length us, event | category | flops | bytes accessed | tf_op | source)
XLA Modules:
  0.0 95.9 jit_solution(3106319266093181272)
XLA Ops:
  1.3 4.5 %parts.1 = (bf16[8,2,128,128]{3,2,1,0:T(8,128)(2,1)}, bf16[16,400,128]{2,1,0:T(8,128)(2,1)}) custom-call(bf16[8,2,128,128]{3,2,1,0:T(8,128)(2,1)} %data.1, f32[2,8]{1,0:T(2,128)} %bitcast.1, s32[1]{0:T(128)S(6)} %copy.8.panel_hbm, bf16[16,2,128,128]{3,2,1,0:T(8,128)(2,1)} %tiles_hbm.1, s32[16]{0:T(128)} %rows_hbm.1, s32[16]{0:T(128)} %freqs.1), custom_call_target="tpu_custom_call" | custom-call | bytes 1048576 | tf_op jit(solution)/shard_map/parts/pallas_call | solution.py:289
  5.8 47.2 %all_to_all.10.parts = bf16[16,400,128]{2,1,0:T(8,128)(2,1)S(1)} all-to-all(bf16[16,400,128]{2,1,0:T(8,128)(2,1)} %get-tuple-element.5), channel_id=1, replica_groups={{0,1,2,3,4,5,6,7,8,9,10,11,12,13,14,15},{16,17,18,19,20,21,22,23,24,25,..., dimensions={0} | all-to-all | bytes 3276800 | tf_op jit(solution)/shard_map/all_to_all | solution.py:279
  52.9 1.1 %residual_slices.1 = bf16[16,384,128]{2,1,0:T(8,128)(2,1)S(1)} custom-call(bf16[16,400,128]{2,1,0:T(8,128)(2,1)S(1)} %all_to_all.10.parts), custom_call_target="tpu_custom_call" | custom-call | bytes 1048576 | tf_op jit(solution)/shard_map/residual_slices/pallas_call | solution.py:313
  54.1 0.0 copy-start
  54.1 0.0 copy-start.1
  54.1 0.0 copy-start.2
  54.1 39.1 %all_to_all.11.arrived = bf16[16,384,128]{2,1,0:T(8,128)(2,1)S(1)} all-to-all(bf16[16,384,128]{2,1,0:T(8,128)(2,1)S(1)} %residual_slices.1), channel_id=1, replica_groups={{0,1,2,3,4,5,6,7,8,9,10,11,12,13,14,15},{16,17,18,19,20,21,22,23,24,25,..., dimensions={0} | all-to-all | bytes 3145728 | tf_op jit(solution)/shard_map/all_to_all | solution.py:279
  93.2 0.0 copy-done
  93.2 0.0 copy-done.1
  93.2 0.0 copy-done.2
  93.2 2.7 %gradient.1 = (f32[8,2,128,128]{3,2,1,0:T(8,128)}, bf16[16,2,128,128]{3,2,1,0:T(8,128)(2,1)}) custom-call(bf16[8,2,128,128]{3,2,1,0:T(8,128)(2,1)S(1)} %copy-done, bf16[8,2,128,128]{3,2,1,0:T(8,128)(2,1)S(1)} %copy-done.1, s32[16]{0:T(128)S(1)} %copy-done.2, bf16[16,384,128]{2,1,0:T(8,128)(2,1)S(1)} %all_to_all.11.arrived), custom_call_target="tpu_custom_call" | custom-call | bytes 1048576 | tf_op jit(solution)/shard_map/gradient/pallas_call | solution.py:337
Async XLA Ops:
  54.1 39.1 %copy-start = (bf16[8,2,128,128]{3,2,1,0:T(8,128)(2,1)S(1)}, bf16[8,2,128,128]{3,2,1,0:T(8,128)(2,1)}, u32[]{:S(2)}) copy-start(bf16[8,2,128,128]{3,2,1,0:T(8,128)(2,1)} %data.1) | copy-start | bytes 1572868
  54.1 39.1 %copy-start.1 = (bf16[8,2,128,128]{3,2,1,0:T(8,128)(2,1)S(1)}, bf16[8,2,128,128]{3,2,1,0:T(8,128)(2,1)}, u32[]{:S(2)}) copy-start(bf16[8,2,128,128]{3,2,1,0:T(8,128)(2,1)} %get-tuple-element.4.source) | copy-start | bytes 1572868
  54.1 39.1 %copy-start.2 = (s32[16]{0:T(128)S(1)}, s32[16]{0:T(128)}, u32[]{:S(2)}) copy-start(s32[16]{0:T(128)} %freqs.1) | copy-start | bytes 196

commit v5 on v4

--- a/solution.py
+++ b/solution.py
@@ -26,6 +26,10 @@
         cost_estimate=pl.CostEstimate(flops=0, bytes_accessed=1 << 20, transcendentals=0),
         compiler_params=pltpu.CompilerParams(vmem_limit_bytes=mib * 1024 * 1024),
     )
+
+
+def stay(array):
+    return pltpu.with_memory_space_constraint(array, pltpu.HBM)
 
 
 def put(buffer, slot, count, real, imag):
@@ -97,7 +101,7 @@
         put(wide, t, slots, real, product[:block, shots:] + product[block:, :shots])
         return carry
 
-    lax.fori_loop(0, slots, one, 0, unroll=4)
+    lax.fori_loop(0, slots, one, 0, unroll=16)
     for j in range(GROUP):
         out[j, :first] = wide[j * first : (j + 1) * first].astype(BF16)
 
@@ -305,8 +309,7 @@
             wide,
             wide_data,
         ],
-        mib=60,
-    )(data, wavelet.T, panel_block, tiles, cover_rows, cover_freqs)
+    )(stay(data), stay(wavelet.T), panel_block, *map(stay, (tiles, cover_rows, cover_freqs)))
     parts = exchange(sent)
     returns = payload(height * (slots + freq_count))
     if groups == 1:

time: 96.5 us -> 94.4 us (0.978)
  Pallas kernels: 8.32 us -> 6.52 us
    pallas_call x1, Pallas kernels: 4.47 us -> 2.68 us  [per_device(): call(parts_kernel, 'parts', [jax.ShapeDtypeStruct(data.shape, BF16), payl...]
where the time goes in v5:
time: 94.4 us; the launch traced here: 93.9 us
  blocking collectives  86 us (91%)
  Pallas kernels  6.52 us (7%)
  between operations  1.31 us (1%)
    all_to_all x2, blocking collectives, exchange(): lax.all_to_all(value, 'tiles', split_axis=0, concat_axis=0, tiled=True, a...  86 us
    pallas_call x1, Pallas kernels, per_device(): call(gradient_kernel, 'gradient', (jax.ShapeDtypeStruct(data.shape, F32),...  2.71 us
    pallas_call x1, Pallas kernels, per_device(): call(parts_kernel, 'parts', [jax.ShapeDtypeStruct(data.shape, BF16), payl...  2.68 us

profile of v5, /device:TPU:0, one launch (start us, length us, event | category | flops | bytes accessed | tf_op | source)
XLA Modules:
  0.0 93.9 jit_solution(13071969140712681994)
XLA Ops:
  1.3 2.7 %parts.1 = (bf16[8,2,128,128]{3,2,1,0:T(8,128)(2,1)S(1)}, bf16[16,400,128]{2,1,0:T(8,128)(2,1)S(1)}) custom-call(bf16[8,2,128,128]{3,2,1,0:T(8,128)(2,1)} %data.1, f32[2,8]{1,0:T(2,128)} %bitcast.1, s32[1]{0:T(128)S(6)} %copy.8.panel_hbm, bf16[16,2,128,128]{3,2,1,0:T(8,128)(2,1)} %tiles_hbm.1, s32[16]{0:T(128)} %rows_hbm.1, s32[16]{0:T(128)} %freqs.1), custom_call_target="tpu_custom_call" | custom-call | bytes 1048576 | tf_op jit(solution)/shard_map/parts/pallas_call | solution.py:293
  4.0 46.9 %all_to_all.10.parts = bf16[16,400,128]{2,1,0:T(8,128)(2,1)S(1)} all-to-all(bf16[16,400,128]{2,1,0:T(8,128)(2,1)S(1)} %get-tuple-element.5), channel_id=1, replica_groups={{0,1,2,3,4,5,6,7,8,9,10,11,12,13,14,15},{16,17,18,19,20,21,22,23,24,25,..., dimensions={0} | all-to-all | bytes 3276800 | tf_op jit(solution)/shard_map/all_to_all | solution.py:283
  50.9 1.1 %residual_slices.1 = bf16[16,384,128]{2,1,0:T(8,128)(2,1)S(1)} custom-call(bf16[16,400,128]{2,1,0:T(8,128)(2,1)S(1)} %all_to_all.10.parts), custom_call_target="tpu_custom_call" | custom-call | bytes 1048576 | tf_op jit(solution)/shard_map/residual_slices/pallas_call | solution.py:316
  52.1 0.0 copy-start
  52.1 0.0 copy-start.1
  52.1 39.1 %all_to_all.11.arrived = bf16[16,384,128]{2,1,0:T(8,128)(2,1)S(1)} all-to-all(bf16[16,384,128]{2,1,0:T(8,128)(2,1)S(1)} %residual_slices.1), channel_id=1, replica_groups={{0,1,2,3,4,5,6,7,8,9,10,11,12,13,14,15},{16,17,18,19,20,21,22,23,24,25,..., dimensions={0} | all-to-all | bytes 3145728 | tf_op jit(solution)/shard_map/all_to_all | solution.py:283
  91.1 0.0 copy-done
  91.1 0.0 copy-done.1
  91.2 2.7 %gradient.1 = (f32[8,2,128,128]{3,2,1,0:T(8,128)}, bf16[16,2,128,128]{3,2,1,0:T(8,128)(2,1)}) custom-call(bf16[8,2,128,128]{3,2,1,0:T(8,128)(2,1)S(1)} %copy-done, bf16[8,2,128,128]{3,2,1,0:T(8,128)(2,1)S(1)} %get-tuple-element.4.source, s32[16]{0:T(128)S(1)} %copy-done.1, bf16[16,384,128]{2,1,0:T(8,128)(2,1)S(1)} %all_to_all.11.arrived), custom_call_target="tpu_custom_call" | custom-call | bytes 1048576 | tf_op jit(solution)/shard_map/gradient/pallas_call | solution.py:340
Async XLA Ops:
  52.1 39.1 %copy-start = (bf16[8,2,128,128]{3,2,1,0:T(8,128)(2,1)S(1)}, bf16[8,2,128,128]{3,2,1,0:T(8,128)(2,1)}, u32[]{:S(2)}) copy-start(bf16[8,2,128,128]{3,2,1,0:T(8,128)(2,1)} %data.1) | copy-start | bytes 1572868
  52.1 39.1 %copy-start.1 = (s32[16]{0:T(128)S(1)}, s32[16]{0:T(128)}, u32[]{:S(2)}) copy-start(s32[16]{0:T(128)} %freqs.1) | copy-start | bytes 196

commit v6 on v0

v6 whole, which is shorter than its diff:
```python
import functools

import jax
import jax.numpy as jnp
from jax import lax
from jax.experimental import pallas as pl
from jax.experimental.pallas import tpu as pltpu
from jax.sharding import PartitionSpec as P

GROUP = 8
CHIPS = (2, 4, 6)
BF16 = jnp.bfloat16
F32 = jnp.float32
VMEM = pl.BlockSpec(memory_space=pltpu.VMEM)
SMEM = pl.BlockSpec(memory_space=pltpu.SMEM)
HBM = pl.BlockSpec(memory_space=pltpu.HBM)
ANY = pl.BlockSpec(memory_space=pl.ANY)


def call(kernel, name, out_shape, in_specs, scratch=(), out_specs=None, mib=24):
    return pl.pallas_call(
        kernel,
        name=name,
        out_shape=out_shape,
        in_specs=in_specs,
        out_specs=out_specs or jax.tree.map(lambda _: VMEM, out_shape),
        scratch_shapes=list(scratch),
        cost_estimate=pl.CostEstimate(flops=0, bytes_accessed=1 << 20, transcendentals=0),
        compiler_params=pltpu.CompilerParams(vmem_limit_bytes=mib * 1024 * 1024),
    )


def stay(array):
    return pltpu.with_memory_space_constraint(array, pltpu.HBM)


def local_index():
    return lax.rem(lax.axis_index("tiles"), GROUP)


def group_index():
    return lax.div(lax.axis_index("tiles"), GROUP)


def put(buffer, slot, count, real, imag):
    piece = real.shape[0] // GROUP
    for j in range(GROUP):
        at = slice(j * piece, (j + 1) * piece)
        first = 2 * j * piece * count + slot
        buffer[pl.ds(first, piece, stride=count), :] = real[at]
        buffer[pl.ds(first + piece * count, piece, stride=count), :] = imag[at]


def transposed_dot(left, right):
    return lax.dot_general(left, right, (((0,), (0,)), ((), ())), preferred_element_type=F32)


def member_rows(k, count):
    return pl.ds(pl.multiple_of((local_index() ^ k) * count, count), count)


def parts_kernel(data_hbm, wavelet_hbm, panel_hbm, tiles_hbm, rows_hbm, freqs_hbm, *refs):
    source, outs = refs[0], refs[1 : 1 + GROUP]
    data, wavelet, panel, tiles, rows, freqs, sems, wide = refs[1 + GROUP :]
    freq_count, _, block, shots = data.shape
    slots = tiles.shape[0]
    size = 2 * block // GROUP * slots
    half = lax.axis_size("tiles") * freq_count // 2
    pairs = (
        (data_hbm, data),
        (tiles_hbm, tiles),
        (wavelet_hbm, wavelet),
        (panel_hbm, panel),
        (freqs_hbm, freqs),
        (rows_hbm, rows),
    )
    copies = [pltpu.make_async_copy(*pair, sems.at[i]) for i, pair in enumerate(pairs)]
    for copy in copies:
        copy.start()
    diagonal = (
        lax.broadcasted_iota(jnp.int32, (block, shots), 0)
        == lax.broadcasted_iota(jnp.int32, (block, shots), 1)
    ).astype(F32)
    for i in (2, 3, 4, 5, 0):
        copies[i].wait()
    identity = diagonal * (lax.axis_index("tiles") == panel[0]).astype(F32)
    for f in range(freq_count):
        source[f, 0] = (wavelet[0, f] * identity - data[f, 0].astype(F32)).astype(BF16)
        source[f, 1] = (wavelet[1, f] * identity - data[f, 1].astype(F32)).astype(BF16)
    line = lax.broadcasted_iota(jnp.int32, (slots, shots), 0)
    targets = jnp.zeros((slots, shots), jnp.int32)
    for t in range(slots):
        targets = jnp.where(line == t, rows[t] * freq_count + freqs[t] - half, targets)
    for k in range(GROUP):
        outs[k][size:] = targets.astype(F32).astype(BF16)
    copies[1].wait()

    def one(t, carry):
        f = freqs[t]
        left = tiles[t].reshape(2 * block, block)
        right = jnp.concatenate([source[f, 0], source[f, 1]], axis=1)
        product = jnp.dot(left, right, preferred_element_type=F32)
        real = product[:block, :shots] - product[block:, shots:]
        put(wide, t, slots, real, product[:block, shots:] + product[block:, :shots])
        return carry

    lax.fori_loop(0, slots, one, 0, unroll=16)
    for k in range(GROUP):
        outs[k][:size] = wide[member_rows(k, size)].astype(BF16)


def sums_kernel(sizes, *refs):
    slots, groups, span, cap = sizes
    parts, (hot_out, own, *sends) = refs[:GROUP], refs[GROUP:]
    height, _, shots = own.shape
    count = GROUP * slots
    group = group_index()
    targets = jnp.concatenate([part[height * slots :] for part in parts], axis=0).astype(F32)
    lane = lax.broadcasted_iota(jnp.int32, (count, shots), 1)
    hot = []
    for q in range(0, groups, shots // span):
        here = jnp.zeros((count, shots), jnp.int32)
        for i in range(shots // span):
            inside = lane - i * span + (group ^ (q + i)) * span - groups * span // 2
            here = jnp.where(lane >= i * span, inside, here)
        hot.append((targets == here.astype(F32)).astype(F32).astype(BF16))
    if groups == 2:
        other = hot[0][:, span:]
        used = (transposed_dot(other, jnp.ones((count, shots), BF16)) > 0).astype(F32)
        before = (
            lax.broadcasted_iota(jnp.int32, (span, span), 0)
            > lax.broadcasted_iota(jnp.int32, (span, span), 1)
        ).astype(F32)
        rank = jnp.dot(before.astype(BF16), used.astype(BF16), preferred_element_type=F32)
        slot = lax.broadcasted_iota(jnp.int32, (span, shots), 1).astype(F32)
        chosen = jnp.where(rank == slot, used, 0.0)
        number = jnp.sum(used, axis=0, keepdims=True)
        sends[0][height * cap :] = jnp.where(slot < span, chosen, number).astype(BF16)
        moved = jnp.dot(other, chosen[:, :span].astype(BF16), preferred_element_type=F32)
        hot = [jnp.concatenate([hot[0][:, :span], moved.astype(BF16)], axis=1)]
    hot = jnp.concatenate(hot, axis=1) if len(hot) > 1 else hot[0]
    hot_out[...] = hot
    step = 2
    for r in range(0, height, step):
        rows = [
            jnp.concatenate([part[(r + i) * slots : (r + i + 1) * slots] for part in parts], axis=0)
            for i in range(step)
        ]
        total = transposed_dot(hot, jnp.concatenate(rows, axis=1))
        for i in range(step):
            values = total[:, i * shots : (i + 1) * shots]
            own[r + i] = values[:span]
            if groups == 2:
                at = slice((r + i) * cap, (r + i + 1) * cap)
                sends[0][at] = values[span : span + cap].astype(BF16)
                sends[1][r + i] = values[span + cap :].astype(BF16)
            else:
                for q, send in enumerate(sends, 1):
                    send[r + i] = values[q * span : (q + 1) * span].astype(BF16)


def hand_out(outs, rows):
    size = outs[0].shape[0]
    outs[0][...] = rows(0)
    outs[1][...] = rows(1)
    for out, k in zip(outs[2:], CHIPS):
        out[:size] = rows(k)
        out[size:] = rows(k ^ 1)


def collect(refs, rows):
    own, *got, mate = refs
    size = own.shape[0]
    rows(0, own[...])
    rows(1, mate[:size])
    for i, k in enumerate(CHIPS):
        rows(k, got[i][:size])
        rows(k ^ 1, mate[(i + 1) * size : (i + 2) * size])


def relay_kernel(own, *refs):
    got, out = refs[:-1], refs[-1]
    size = own.shape[0]
    out[:size] = own[...]
    for i, ref in enumerate(got, 1):
        out[i * size : (i + 1) * size] = ref[size:]


def most_kernel(got_hbm, mine_hbm, *refs):
    out, got, mine, sems = refs[-4:]
    last = pl.ds(got_hbm.shape[0] - got.shape[0], got.shape[0])
    copies = [
        pltpu.make_async_copy(got_hbm.at[last], got, sems.at[0]),
        pltpu.make_async_copy(mine_hbm.at[last], mine, sems.at[1]),
    ]
    for copy in copies:
        copy.start()
    for copy in copies:
        copy.wait()
    half = got.shape[1] // 2
    most = jnp.maximum(got[:, half:].astype(F32), mine[:, half:].astype(F32))
    out[0] = jnp.max(most).astype(jnp.int32)


def slices_kernel(data, _, *refs):
    outs, wide = refs[:-1], refs[-1]
    freq_count = data.shape[0]
    for f in range(freq_count):
        put(wide, f, freq_count, data[f, 0].astype(F32), data[f, 1].astype(F32))
    for k in range(GROUP):
        outs[k][...] = wide[member_rows(k, outs[k].shape[0])].astype(BF16)


def residual_kernel(sizes, own, *refs):
    slots, groups, span, cap = sizes
    height, _, shots = own.shape
    data_in, refs = refs[:GROUP], refs[GROUP:]
    if groups == 2:
        got, got_rest, rounded, send, rest, *outs, data, back = refs
        chosen = got[height * cap :, :span]
    else:
        got, (rounded, *outs, data, back) = refs[: groups - 1], refs[groups - 1 :]
    local = local_index()
    freq_count = data.shape[1] // height
    for k in range(GROUP):
        data[local ^ k] = data_in[k][...]
    step = 8
    for r in range(0, height, step):
        rows = range(r, r + step)
        total = jnp.concatenate([own[i] for i in rows], axis=1)
        if groups == 2:
            more = []
            for i in rows:
                used = got[i * cap : (i + 1) * cap]
                more.append(jnp.concatenate([used, got_rest[i]], axis=0))
            more = jnp.concatenate(more, axis=1)
            total += jnp.dot(chosen, more, preferred_element_type=F32)
        else:
            for ref in got:
                total += jnp.concatenate([ref[i].astype(F32) for i in rows], axis=1)
        values = data[:, r * freq_count : (r + step) * freq_count].astype(F32)
        values = [
            values[:, i * freq_count : (i + 1) * freq_count].reshape(span, shots)
            for i in range(step)
        ]
        values = (jnp.concatenate(values, axis=1) - total).astype(BF16)
        for j in range(GROUP):
            at = slice(j * freq_count, (j + 1) * freq_count)
            pair = [total[at, i * shots : (i + 1) * shots] for i in range(step)]
            pair = jnp.concatenate(pair, axis=0)
            back[j, r * freq_count : (r + step) * freq_count] = pair.astype(BF16)
        picked = transposed_dot(chosen, values).astype(BF16) if groups == 2 else None
        for i in rows:
            at = slice((i - r) * shots, (i - r + 1) * shots)
            rounded[i] = values[:, at]
            if groups == 2:
                send[i] = picked[:cap, at]
                rest[i] = picked[cap:, at]
    hand_out(outs, lambda k: back[local ^ k])


def spread_kernel(slots, hot, *refs):
    have, outs = refs[:-GROUP], refs[-GROUP:]
    height, _, shots = have[0].shape
    step = 8
    for r in range(0, height, step):
        rows = [
            jnp.concatenate([ref[i] for ref in have], axis=0) for i in range(r, r + step)
        ]
        picked = jnp.dot(hot[...], jnp.concatenate(rows, axis=1), preferred_element_type=F32)
        picked = picked.astype(BF16)
        for i in range(step):
            for k in range(GROUP):
                outs[k][(r + i) * slots : (r + i + 1) * slots] = picked[
                    k * slots : (k + 1) * slots, i * shots : (i + 1) * shots
                ]


def residual_out_kernel(data, *refs):
    back, (residual, wide) = refs[:-2], refs[-2:]
    freq_count, _, block, _ = data.shape
    size = back[0].shape[0]
    piece = block // GROUP

    def keep(k, rows):
        wide[member_rows(k, size)] = rows.astype(F32)

    collect(back, keep)
    for f in range(freq_count):
        real, imag = data[f, 0].astype(F32), data[f, 1].astype(F32)
        for j in range(GROUP):
            at = slice(j * piece, (j + 1) * piece)
            first = j * size + f
            rows = pl.ds(first, piece, stride=freq_count)
            residual[f, 0, at, :] = real[at] - wide[rows, :]
            rows = pl.ds(first + piece * freq_count, piece, stride=freq_count)
            residual[f, 1, at, :] = imag[at] - wide[rows, :]


def gradient_kernel(source, freqs_hbm, *refs):
    parts, (gradient_hbm, gradient, wide, freqs, sems) = refs[:GROUP], refs[GROUP:]
    copy = pltpu.make_async_copy(freqs_hbm, freqs, sems.at[4])
    copy.start()
    slots, _, block, _ = gradient.shape
    size, shots = parts[0].shape
    height = size // slots
    piece = height // 2
    scale = 1.0 / shots
    for k in range(GROUP):
        wide[member_rows(k, size)] = parts[k][...].astype(F32)
    copy.wait()

    def one(t, carry):
        left = wide[pl.ds(t, GROUP * height, stride=slots), :].astype(BF16)
        right = source[freqs[t]].reshape(2 * block, shots)
        total = -scale * lax.dot_general(
            left, right, (((1,), (1,)), ((), ())), preferred_element_type=F32
        )
        real, imag = [], []
        for j in range(GROUP):
            upper = total[j * height : j * height + piece]
            lower = total[j * height + piece : (j + 1) * height]
            real.append(upper[:, :block] + lower[:, block:])
            imag.append(lower[:, :block] - upper[:, block:])
        gradient[t, 0] = jnp.concatenate(real, axis=0).astype(BF16)
        gradient[t, 1] = jnp.concatenate(imag, axis=0).astype(BF16)
        return carry

    copies = []
    quarters = 4
    step = slots // quarters
    for i in range(quarters):
        lax.fori_loop(i * step, (i + 1) * step, one, 0, unroll=4)
        at = pl.ds(i * step, step)
        copies.append(
            pltpu.make_async_copy(gradient.at[at], gradient_hbm.at[at], sems.at[i])
        )
        copies[-1].start()
    for copy in copies:
        copy.wait()


def per_device(data, wavelet, panel_block, tiles, cover_rows, cover_freqs):
    freq_count, _, block, shots = data.shape
    slots = tiles.shape[0]
    peers = lax.axis_size("tiles")
    groups = peers // GROUP
    height = 2 * block // GROUP
    span = GROUP * freq_count
    cap = 3 * span // 4 if groups == 2 else span
    sizes = (slots, groups, span, cap)

    def shape(*dims, kind=BF16):
        return jax.ShapeDtypeStruct((*dims, shots), kind)

    wide = pltpu.VMEM((GROUP * height * slots, shots), F32)
    wide_data = pltpu.VMEM((GROUP * height * freq_count, shots), F32)
    to_members = [jax.ShapeDtypeStruct((height * slots, shots), BF16)] * GROUP
    size = height * freq_count
    to_owners = [shape(size)] * 2 + [shape(2 * size)] * len(CHIPS)
    members = pltpu.VMEM((GROUP, height * freq_count, shots), BF16)

    def swap(value, distance):
        return lax.ppermute(value, "tiles", [(i, i ^ distance) for i in range(peers)])

    def in_group(values):
        got = {k: swap(values[k], k) for k in (6, 4, 2, 7, 5, 3, 1)}
        return [values[0]] + [got[k] for k in range(1, GROUP)]

    def hand_around(values):
        got = [swap(value, k) for value, k in zip(values[2:], CHIPS)]
        mate = call(relay_kernel, "for_mate", shape(4 * size), [VMEM] * (1 + len(CHIPS)))(
            values[1], *got
        )
        return [values[0], *got, swap(mate, 1)]

    def across(values):
        return [swap(value, q * GROUP) for q, value in enumerate(values, 1)]

    source, *sent = call(
        parts_kernel,
        "parts",
        [shape(freq_count, 2, block)] + [shape(height * slots + slots)] * GROUP,
        [HBM] * 6,
        scratch=[
            pltpu.VMEM(data.shape, BF16),
            pltpu.SMEM((2, freq_count), F32),
            pltpu.SMEM((1,), jnp.int32),
            pltpu.VMEM(tiles.shape, BF16),
            pltpu.SMEM((slots,), jnp.int32),
            pltpu.SMEM((slots,), jnp.int32),
            pltpu.SemaphoreType.DMA((6,)),
            wide,
        ],
    )(stay(data), stay(wavelet.T), panel_block, *map(stay, (tiles, cover_rows, cover_freqs)))
    rests = [shape(height, span - cap)] if groups == 2 else []
    if groups == 2:
        sends = [shape(height * cap + span)]
    else:
        sends = [shape(height, span)] * (groups - 1)
    hot, own, *out = call(
        functools.partial(sums_kernel, sizes),
        "sums",
        [
            jax.ShapeDtypeStruct((GROUP * slots, groups * span), BF16),
            shape(height, span, kind=F32),
        ]
        + sends
        + rests,
        [VMEM] * GROUP,
    )(*in_group(sent))
    got = [swap(out[0], GROUP)] if groups == 2 else across(out)
    data_in = in_group(
        call(slices_kernel, "data_slices", [shape(size)] * GROUP, [VMEM, ANY], scratch=[wide_data])(
            data, own
        )
    )
    if groups == 2:
        most = call(
            most_kernel,
            "most",
            jax.ShapeDtypeStruct((1,), jnp.int32),
            [ANY] * (2 + GROUP - 1),
            out_specs=SMEM,
            scratch=[pltpu.VMEM((16, shots), BF16)] * 2 + [pltpu.SemaphoreType.DMA((2,))],
        )(got[0], out[0], *data_in[1:])
        full = most[0] > cap

        def rest(value):
            return lax.cond(full, lambda v: swap(v, GROUP), jnp.zeros_like, value)

        got.append(rest(out[1]))
    rounded, *out = call(
        functools.partial(residual_kernel, sizes),
        "residual_slices",
        [shape(height, span)] + ([shape(height, cap)] + rests if groups == 2 else []) + to_owners,
        [VMEM] * (1 + len(data_in) + len(got)),
        scratch=[members, members],
    )(own, *data_in, *got)
    if groups == 2:
        got = [swap(out[0], GROUP), rest(out[1])]
    else:
        got = across([rounded] * (groups - 1))
    residual = call(
        residual_out_kernel,
        "residual",
        jax.ShapeDtypeStruct(data.shape, F32),
        [VMEM] * (1 + len(to_owners)),
        scratch=[wide_data],
    )(data, *hand_around(out[-len(to_owners) :]))
    out = call(
        functools.partial(spread_kernel, slots),
        "spread",
        to_members,
        [VMEM] * (2 + len(got)),
    )(hot, rounded, *got)
    gradient = call(
        gradient_kernel,
        "gradient",
        jax.ShapeDtypeStruct(tiles.shape, BF16),
        [VMEM, HBM] + [VMEM] * GROUP,
        out_specs=HBM,
        scratch=[
            pltpu.VMEM(tiles.shape, BF16),
            wide,
            pltpu.SMEM((slots,), jnp.int32),
            pltpu.SemaphoreType.DMA((5,)),
        ],
    )(source, stay(cover_freqs), *in_group(out))
    return residual, gradient


def solution(mesh):
    in_specs = (
        P("windows", None, "tiles", None),
        P(),
        P(),
        P(("windows", "tiles"), None, None, None),
        P(("windows", "tiles")),
        P(("windows", "tiles")),
    )
    out_specs = (P("windows", None, "tiles", None), P(("windows", "tiles"), None, None, None))
    return jax.shard_map(
        per_device, mesh=mesh, in_specs=in_specs, out_specs=out_specs, check_vma=False
    )
```

time: 139 us -> 91.4 us (0.66)
  the two profiles are of different devices: /device:TPU:15 before, /device:TPU:0 now
where the time goes in v6:
time: 91.4 us; the launch traced here: 90.9 us
  waiting for transfers between devices  45.8 us (50%)
  starting transfers between devices  26.7 us (29%)
  Pallas kernels  12.8 us (14%)
  local copies, waits for them, and re-layouts  3.58 us (4%)
  between operations  2.02 us (2%)
    ppermute x27, waiting for transfers between devices, swap(): lax.ppermute(value, 'tiles', [(i, i ^ distance) for i in range(peers)])  45.8 us
    ppermute x27, starting transfers between devices, swap(): lax.ppermute(value, 'tiles', [(i, i ^ distance) for i in range(peers)])  26.7 us
    pallas_call x1, Pallas kernels, per_device(): call(parts_kernel, 'parts', [shape(freq_count, 2, block)] + [shape(height...  2.63 us
    pallas_call x1, Pallas kernels, per_device(): call(functools.partial(residual_kernel, sizes), 'residual_slices', [shape...  2.56 us
    pallas_call x1, Pallas kernels, per_device(): call(gradient_kernel, 'gradient', jax.ShapeDtypeStruct(tiles.shape, BF16)...  2.3 us
    unnamed x12, local copies, waits for them, and re-layouts  2.25 us
  transfers between devices with their start and end apart: 27, of which 18 were waited for; matrix products, arithmetic and copies ran while one was open for 1% of the time, Pallas kernels for 3%

profile of v6, /device:TPU:0, one launch (start us, length us, event | category | flops | bytes accessed | tf_op | source)
XLA Modules:
  0.0 90.9 jit_solution(14001799792303964578)
XLA Ops:
  1.3 2.6 %parts.1 = (bf16[8,2,128,128]{3,2,1,0:T(8,128)(2,1)S(1)}, bf16[528,128]{1,0:T(8,128)(2,1)S(1)}, bf16[528,128]{1,0:T(8,128)(2,1)S(1)}, bf16[528,128]{1,0:T(8,128)...) custom-call(bf16[8,2,128,128]{3,2,1,0:T(8,128)(2,1)} %data.3, ...), custom_call_target="tpu_custom_call" | custom-call | bytes 1048576 | tf_op jit(solution)/shard_map/parts/pallas_call | solution.py:380
  4.4 2.6 %collective-permute-start.3 = (bf16[528,128]{1,0:T(8,128)(2,1)S(1)}, bf16[528,128]{1,0:T(8,128)(2,1)S(1)}, u32[]{:S(2)}, u32[]{:S(2)}) collective-permute-start(bf16[528,128]{1,0:T(8,128)(2,1)S(1)} %get-tuple-element.49), channel_id=1, source_target_pairs={{0,2},{1,3},{2,0},{3,1},{4,6},{5,7},{6,4},{7,5},{8,10},{9,11},{10,... | collective-permute-start | bytes 405512 | tf_op jit(solution)/shard_map/ppermute | solution.py:364
  7.1 1.8 %collective-permute-start.5 = (bf16[528,128]{1,0:T(8,128)(2,1)S(1)}, bf16[528,128]{1,0:T(8,128)(2,1)S(1)}, u32[]{:S(2)}, u32[]{:S(2)}) collective-permute-start(bf16[528,128]{1,0:T(8,128)(2,1)S(1)} %get-tuple-element.51), channel_id=1, source_target_pairs={{0,4},{1,5},{2,6},{3,7},{4,0},{5,1},{6,2},{7,3},{8,12},{9,13},{10,... | collective-permute-start | bytes 405512 | tf_op jit(solution)/shard_map/ppermute | solution.py:364
  8.9 2.6 %collective-permute-start.7 = (bf16[528,128]{1,0:T(8,128)(2,1)S(1)}, bf16[528,128]{1,0:T(8,128)(2,1)S(1)}, u32[]{:S(2)}, u32[]{:S(2)}) collective-permute-start(bf16[528,128]{1,0:T(8,128)(2,1)S(1)} %get-tuple-element.53), channel_id=1, source_target_pairs={{0,6},{1,7},{2,4},{3,5},{4,2},{5,3},{6,0},{7,1},{8,14},{9,15},{10,... | collective-permute-start | bytes 405512 | tf_op jit(solution)/shard_map/ppermute | solution.py:364
  11.5 1.7 %collective-permute-start.8 = (bf16[528,128]{1,0:T(8,128)(2,1)S(1)}, bf16[528,128]{1,0:T(8,128)(2,1)S(1)}, u32[]{:S(2)}, u32[]{:S(2)}) collective-permute-start(bf16[528,128]{1,0:T(8,128)(2,1)S(1)} %get-tuple-element.54), channel_id=1, source_target_pairs={{0,7},{1,6},{2,5},{3,4},{4,3},{5,2},{6,1},{7,0},{8,15},{9,14},{10,... | collective-permute-start | bytes 405512 | tf_op jit(solution)/shard_map/ppermute | solution.py:364
  13.8 1.9 %collective-permute-done.6.refs_5_ = bf16[528,128]{1,0:T(8,128)(2,1)S(1)} collective-permute-done((bf16[528,128]{1,0:T(8,128)(2,1)S(1)}, bf16[528,128]{1,0:T(8,128)(2,1)S(1)}, u32[]{:S(2)}, u32[]{:S(2)}) %collective-permute-start.6) | collective-permute-done | bytes 135200 | tf_op jit(solution)/shard_map/ppermute | solution.py:364
  15.7 4.7 %collective-permute-done.7.refs_6_ = bf16[528,128]{1,0:T(8,128)(2,1)S(1)} collective-permute-done((bf16[528,128]{1,0:T(8,128)(2,1)S(1)}, bf16[528,128]{1,0:T(8,128)(2,1)S(1)}, u32[]{:S(2)}, u32[]{:S(2)}) %collective-permute-start.7) | collective-permute-done | bytes 135200 | tf_op jit(solution)/shard_map/ppermute | solution.py:364
  20.5 1.8 %collective-permute-done.8.refs_7_ = bf16[528,128]{1,0:T(8,128)(2,1)S(1)} collective-permute-done((bf16[528,128]{1,0:T(8,128)(2,1)S(1)}, bf16[528,128]{1,0:T(8,128)(2,1)S(1)}, u32[]{:S(2)}, u32[]{:S(2)}) %collective-permute-start.8) | collective-permute-done | bytes 135200 | tf_op jit(solution)/shard_map/ppermute | solution.py:364
  22.2 1.7 %sums.1 = (bf16[128,128]{1,0:T(8,128)(2,1)S(1)}, f32[32,64,128]{2,1,0:T(8,128)S(1)}, bf16[1600,128]{1,0:T(8,128)(2,1)S(1)}, bf16[32,16,128]{2,1,0:T(8,128)(2,1)}) custom-call(bf16[528,128]{1,0:T(8,128)(2,1)S(1)} %get-tuple-element.47.refs_0_, bf16[528,128]{1,0:T(8,128)(2,1)S(1)} %collective-permute-done.2.refs_1_, ...), custom_call_target="tpu_custom_call" | custom-call | bytes 1048576 | tf_op jit(solution)/shard_map/sums/pallas_call | solution.py:401
  24.5 2.6 %collective-permute-start.16 = (bf16[1600,128]{1,0:T(8,128)(2,1)S(1)}, bf16[1600,128]{1,0:T(8,128)(2,1)S(1)}, u32[]{:S(2)}, u32[]{:S(2)}) collective-permute-start(bf16[1600,128]{1,0:T(8,128)(2,1)S(1)} %get-tuple-element.64.mine_hbm), channel_id=1, source_target_pairs={{0,8},{1,9},{2,10},{3,11},{4,12},{5,13},{6,14},{7,15},{8,0},{9,1},... | collective-permute-start | bytes 1228808 | tf_op jit(solution)/shard_map/ppermute | solution.py:364
  29.4 1.6 %collective-permute-start.12 = (bf16[256,128]{1,0:T(8,128)(2,1)S(1)}, bf16[256,128]{1,0:T(8,128)(2,1)S(1)}, u32[]{:S(2)}, u32[]{:S(2)}) collective-permute-start(bf16[256,128]{1,0:T(8,128)(2,1)S(1)} %get-tuple-element.60), channel_id=1, source_target_pairs={{0,4},{1,5},{2,6},{3,7},{4,0},{5,1},{6,2},{7,3},{8,12},{9,13},{10,... | collective-permute-start | bytes 196616 | tf_op jit(solution)/shard_map/ppermute | solution.py:364
  34.8 3.6 %collective-permute-done.12.refs_3_.refs_4_ = bf16[256,128]{1,0:T(8,128)(2,1)S(1)} collective-permute-done((bf16[256,128]{1,0:T(8,128)(2,1)S(1)}, bf16[256,128]{1,0:T(8,128)(2,1)S(1)}, u32[]{:S(2)}, u32[]{:S(2)}) %collective-permute-start.12) | collective-permute-done | bytes 65568 | tf_op jit(solution)/shard_map/ppermute | solution.py:364
  41.2 5.2 %collective-permute-done.15.refs_6_.refs_7_ = bf16[256,128]{1,0:T(8,128)(2,1)S(1)} collective-permute-done((bf16[256,128]{1,0:T(8,128)(2,1)S(1)}, bf16[256,128]{1,0:T(8,128)(2,1)S(1)}, u32[]{:S(2)}, u32[]{:S(2)}) %collective-permute-start.15) | collective-permute-done | bytes 65568 | tf_op jit(solution)/shard_map/ppermute | solution.py:364
  49.2 2.6 %residual_slices.1 = (bf16[32,64,128]{2,1,0:T(8,128)(2,1)S(1)}, bf16[32,48,128]{2,1,0:T(8,128)(2,1)}, bf16[32,16,128]{2,1,0:T(8,128)(2,1)}, bf16[256,128]{1,0:T(...) custom-call(f32[32,64,128]{2,1,0:T(8,128)S(1)} %get-tuple-element.55, ...), custom_call_target="tpu_custom_call" | custom-call | bytes 1048576 | tf_op jit(solution)/shard_map/residual_slices/pallas_call | solution.py:433
  53.1 2.8 %collective-permute-start.18 = (bf16[512,128]{1,0:T(8,128)(2,1)S(1)}, bf16[512,128]{1,0:T(8,128)(2,1)S(1)}, u32[]{:S(2)}, u32[]{:S(2)}) collective-permute-start(bf16[512,128]{1,0:T(8,128)(2,1)S(1)} %get-tuple-element.68), channel_id=1, source_target_pairs={{0,4},{1,5},{2,6},{3,7},{4,0},{5,1},{6,2},{7,3},{8,12},{9,13},{10,... | collective-permute-start | bytes 393224 | tf_op jit(solution)/shard_map/ppermute | solution.py:364
  57.3 7.0 %collective-permute-done.18.refs_1_.refs_2_ = bf16[512,128]{1,0:T(8,128)(2,1)S(1)} collective-permute-done((bf16[512,128]{1,0:T(8,128)(2,1)S(1)}, bf16[512,128]{1,0:T(8,128)(2,1)S(1)}, u32[]{:S(2)}, u32[]{:S(2)}) %collective-permute-start.18) | collective-permute-done | bytes 131104 | tf_op jit(solution)/shard_map/ppermute | solution.py:364
  64.3 2.3 %collective-permute-done.19.refs_2_.refs_3_ = bf16[512,128]{1,0:T(8,128)(2,1)S(1)} collective-permute-done((bf16[512,128]{1,0:T(8,128)(2,1)S(1)}, bf16[512,128]{1,0:T(8,128)(2,1)S(1)}, u32[]{:S(2)}, u32[]{:S(2)}) %collective-permute-start.19) | collective-permute-done | bytes 131104 | tf_op jit(solution)/shard_map/ppermute | solution.py:364
  68.2 4.3 %collective-permute-done.21.refs_1_ = bf16[32,48,128]{2,1,0:T(8,128)(2,1)S(1)} collective-permute-done((bf16[32,48,128]{2,1,0:T(8,128)(2,1)}, bf16[32,48,128]{2,1,0:T(8,128)(2,1)S(1)}, u32[]{:S(2)}, u32[]{:S(2)}) %collective-permute-start.21) | collective-permute-done | bytes 393248 | tf_op jit(solution)/shard_map/ppermute | solution.py:364
  74.0 1.8 %collective-permute-start.24 = (bf16[512,128]{1,0:T(8,128)(2,1)S(1)}, bf16[512,128]{1,0:T(8,128)(2,1)S(1)}, u32[]{:S(2)}, u32[]{:S(2)}) collective-permute-start(bf16[512,128]{1,0:T(8,128)(2,1)S(1)} %get-tuple-element.79), channel_id=1, source_target_pairs={{0,3},{1,2},{2,1},{3,0},{4,7},{5,6},{6,5},{7,4},{8,11},{9,10},{10,... | collective-permute-start | bytes 393224 | tf_op jit(solution)/shard_map/ppermute | solution.py:364
  75.7 1.7 %collective-permute-start.26 = (bf16[512,128]{1,0:T(8,128)(2,1)S(1)}, bf16[512,128]{1,0:T(8,128)(2,1)S(1)}, u32[]{:S(2)}, u32[]{:S(2)}) collective-permute-start(bf16[512,128]{1,0:T(8,128)(2,1)S(1)} %get-tuple-element.81), channel_id=1, source_target_pairs={{0,5},{1,4},{2,7},{3,6},{4,1},{5,0},{6,3},{7,2},{8,13},{9,12},{10,... | collective-permute-start | bytes 393224 | tf_op jit(solution)/shard_map/ppermute | solution.py:364
  77.6 2.7 %collective-permute-done.23.refs_2_ = bf16[512,128]{1,0:T(8,128)(2,1)S(1)} collective-permute-done((bf16[512,128]{1,0:T(8,128)(2,1)S(1)}, bf16[512,128]{1,0:T(8,128)(2,1)S(1)}, u32[]{:S(2)}, u32[]{:S(2)}) %collective-permute-start.23) | collective-permute-done | bytes 131104 | tf_op jit(solution)/shard_map/ppermute | solution.py:364
  82.1 1.6 %collective-permute-done.26.refs_5_ = bf16[512,128]{1,0:T(8,128)(2,1)S(1)} collective-permute-done((bf16[512,128]{1,0:T(8,128)(2,1)S(1)}, bf16[512,128]{1,0:T(8,128)(2,1)S(1)}, u32[]{:S(2)}, u32[]{:S(2)}) %collective-permute-start.26) | collective-permute-done | bytes 131104 | tf_op jit(solution)/shard_map/ppermute | solution.py:364
  83.7 3.7 %collective-permute-done.27.refs_6_ = bf16[512,128]{1,0:T(8,128)(2,1)S(1)} collective-permute-done((bf16[512,128]{1,0:T(8,128)(2,1)S(1)}, bf16[512,128]{1,0:T(8,128)(2,1)S(1)}, u32[]{:S(2)}, u32[]{:S(2)}) %collective-permute-start.27) | collective-permute-done | bytes 131104 | tf_op jit(solution)/shard_map/ppermute | solution.py:364
  88.6 2.3 %gradient.1 = bf16[16,2,128,128]{3,2,1,0:T(8,128)(2,1)} custom-call(bf16[8,2,128,128]{3,2,1,0:T(8,128)(2,1)S(1)} %get-tuple-element.71.source, s32[16]{0:T(128)} %freqs_hbm.3, bf16[512,128]{1,0:T(8,128)(2,1)S(1)} %get-tuple-element.76.refs_0_, bf16[512,128]{1,0:T(8,128)(2,1)S(1)} %collective-permute-done.22.refs_1_, ...), custom_call_target="tpu_custom_call" | custom-call | bytes 1048576 | tf_op jit(solution)/shard_map/gradient/pallas_call | solution.py:457
  (55 shorter events, 23.2 us)
Async XLA Ops:
  3.9 5.0 %collective-permute-start.2 = (bf16[528,128]{1,0:T(8,128)(2,1)S(1)}, bf16[528,128]{1,0:T(8,128)(2,1)S(1)}, u32[]{:S(2)}, u32[]{:S(2)}) collective-permute-start(bf16[528,128]{1,0:T(8,128)(2,1)S(1)} %get-tuple-element.48), channel_id=1, source_target_pairs={{0,1},{1,0},{2,3},{3,2},{4,5},{5,4},{6,7},{7,6},{8,9},{9,8},{10,11... | collective-permute-start | bytes 405512 | tf_op jit(solution)/shard_map/ppermute | solution.py:364
  4.4 7.1 %collective-permute-start.3 = (bf16[528,128]{1,0:T(8,128)(2,1)S(1)}, bf16[528,128]{1,0:T(8,128)(2,1)S(1)}, u32[]{:S(2)}, u32[]{:S(2)}) collective-permute-start(bf16[528,128]{1,0:T(8,128)(2,1)S(1)} %get-tuple-element.49), channel_id=1, source_target_pairs={{0,2},{1,3},{2,0},{3,1},{4,6},{5,7},{6,4},{7,5},{8,10},{9,11},{10,... | collective-permute-start | bytes 405512 | tf_op jit(solution)/shard_map/ppermute | solution.py:364
  7.0 6.8 %collective-permute-start.4 = (bf16[528,128]{1,0:T(8,128)(2,1)S(1)}, bf16[528,128]{1,0:T(8,128)(2,1)S(1)}, u32[]{:S(2)}, u32[]{:S(2)}) collective-permute-start(bf16[528,128]{1,0:T(8,128)(2,1)S(1)} %get-tuple-element.50), channel_id=1, source_target_pairs={{0,3},{1,2},{2,1},{3,0},{4,7},{5,6},{6,5},{7,4},{8,11},{9,10},{10,... | collective-permute-start | bytes 405512 | tf_op jit(solution)/shard_map/ppermute | solution.py:364
  7.1 6.7 %collective-permute-start.5 = (bf16[528,128]{1,0:T(8,128)(2,1)S(1)}, bf16[528,128]{1,0:T(8,128)(2,1)S(1)}, u32[]{:S(2)}, u32[]{:S(2)}) collective-permute-start(bf16[528,128]{1,0:T(8,128)(2,1)S(1)} %get-tuple-element.51), channel_id=1, source_target_pairs={{0,4},{1,5},{2,6},{3,7},{4,0},{5,1},{6,2},{7,3},{8,12},{9,13},{10,... | collective-permute-start | bytes 405512 | tf_op jit(solution)/shard_map/ppermute | solution.py:364
  8.9 6.8 %collective-permute-start.6 = (bf16[528,128]{1,0:T(8,128)(2,1)S(1)}, bf16[528,128]{1,0:T(8,128)(2,1)S(1)}, u32[]{:S(2)}, u32[]{:S(2)}) collective-permute-start(bf16[528,128]{1,0:T(8,128)(2,1)S(1)} %get-tuple-element.52), channel_id=1, source_target_pairs={{0,5},{1,4},{2,7},{3,6},{4,1},{5,0},{6,3},{7,2},{8,13},{9,12},{10,... | collective-permute-start | bytes 405512 | tf_op jit(solution)/shard_map/ppermute | solution.py:364
  8.9 11.6 %collective-permute-start.7 = (bf16[528,128]{1,0:T(8,128)(2,1)S(1)}, bf16[528,128]{1,0:T(8,128)(2,1)S(1)}, u32[]{:S(2)}, u32[]{:S(2)}) collective-permute-start(bf16[528,128]{1,0:T(8,128)(2,1)S(1)} %get-tuple-element.53), channel_id=1, source_target_pairs={{0,6},{1,7},{2,4},{3,5},{4,2},{5,3},{6,0},{7,1},{8,14},{9,15},{10,... | collective-permute-start | bytes 405512 | tf_op jit(solution)/shard_map/ppermute | solution.py:364
  11.5 10.7 %collective-permute-start.8 = (bf16[528,128]{1,0:T(8,128)(2,1)S(1)}, bf16[528,128]{1,0:T(8,128)(2,1)S(1)}, u32[]{:S(2)}, u32[]{:S(2)}) collective-permute-start(bf16[528,128]{1,0:T(8,128)(2,1)S(1)} %get-tuple-element.54), channel_id=1, source_target_pairs={{0,7},{1,6},{2,5},{3,4},{4,3},{5,2},{6,1},{7,0},{8,15},{9,14},{10,... | collective-permute-start | bytes 405512 | tf_op jit(solution)/shard_map/ppermute | solution.py:364
  24.5 21.9 %collective-permute-start.16 = (bf16[1600,128]{1,0:T(8,128)(2,1)S(1)}, bf16[1600,128]{1,0:T(8,128)(2,1)S(1)}, u32[]{:S(2)}, u32[]{:S(2)}) collective-permute-start(bf16[1600,128]{1,0:T(8,128)(2,1)S(1)} %get-tuple-element.64.mine_hbm), channel_id=1, source_target_pairs={{0,8},{1,9},{2,10},{3,11},{4,12},{5,13},{6,14},{7,15},{8,0},{9,1},... | collective-permute-start | bytes 1228808 | tf_op jit(solution)/shard_map/ppermute | solution.py:364
  28.1 5.5 %collective-permute-start.11 = (bf16[256,128]{1,0:T(8,128)(2,1)S(1)}, bf16[256,128]{1,0:T(8,128)(2,1)S(1)}, u32[]{:S(2)}, u32[]{:S(2)}) collective-permute-start(bf16[256,128]{1,0:T(8,128)(2,1)S(1)} %get-tuple-element.59), channel_id=1, source_target_pairs={{0,3},{1,2},{2,1},{3,0},{4,7},{5,6},{6,5},{7,4},{8,11},{9,10},{10,... | collective-permute-start | bytes 196616 | tf_op jit(solution)/shard_map/ppermute | solution.py:364
  29.4 9.0 %collective-permute-start.12 = (bf16[256,128]{1,0:T(8,128)(2,1)S(1)}, bf16[256,128]{1,0:T(8,128)(2,1)S(1)}, u32[]{:S(2)}, u32[]{:S(2)}) collective-permute-start(bf16[256,128]{1,0:T(8,128)(2,1)S(1)} %get-tuple-element.60), channel_id=1, source_target_pairs={{0,4},{1,5},{2,6},{3,7},{4,0},{5,1},{6,2},{7,3},{8,12},{9,13},{10,... | collective-permute-start | bytes 196616 | tf_op jit(solution)/shard_map/ppermute | solution.py:364
  31.0 8.8 %collective-permute-start.13 = (bf16[256,128]{1,0:T(8,128)(2,1)S(1)}, bf16[256,128]{1,0:T(8,128)(2,1)S(1)}, u32[]{:S(2)}, u32[]{:S(2)}) collective-permute-start(bf16[256,128]{1,0:T(8,128)(2,1)S(1)} %get-tuple-element.61), channel_id=1, source_target_pairs={{0,5},{1,4},{2,7},{3,6},{4,1},{5,0},{6,3},{7,2},{8,13},{9,12},{10,... | collective-permute-start | bytes 196616 | tf_op jit(solution)/shard_map/ppermute | solution.py:364
  32.5 8.7 %collective-permute-start.14 = (bf16[256,128]{1,0:T(8,128)(2,1)S(1)}, bf16[256,128]{1,0:T(8,128)(2,1)S(1)}, u32[]{:S(2)}, u32[]{:S(2)}) collective-permute-start(bf16[256,128]{1,0:T(8,128)(2,1)S(1)} %get-tuple-element.62), channel_id=1, source_target_pairs={{0,6},{1,7},{2,4},{3,5},{4,2},{5,3},{6,0},{7,1},{8,14},{9,15},{10,... | collective-permute-start | bytes 196616 | tf_op jit(solution)/shard_map/ppermute | solution.py:364
  33.6 12.8 %collective-permute-start.15 = (bf16[256,128]{1,0:T(8,128)(2,1)S(1)}, bf16[256,128]{1,0:T(8,128)(2,1)S(1)}, u32[]{:S(2)}, u32[]{:S(2)}) collective-permute-start(bf16[256,128]{1,0:T(8,128)(2,1)S(1)} %get-tuple-element.63), channel_id=1, source_target_pairs={{0,7},{1,6},{2,5},{3,4},{4,3},{5,2},{6,1},{7,0},{8,15},{9,14},{10,... | collective-permute-start | bytes 196616 | tf_op jit(solution)/shard_map/ppermute | solution.py:364
  51.8 20.7 %collective-permute-start.21 = (bf16[32,48,128]{2,1,0:T(8,128)(2,1)}, bf16[32,48,128]{2,1,0:T(8,128)(2,1)S(1)}, u32[]{:S(2)}, u32[]{:S(2)}) collective-permute-start(bf16[32,48,128]{2,1,0:T(8,128)(2,1)} %get-tuple-element.74), channel_id=1, source_target_pairs={{0,8},{1,9},{2,10},{3,11},{4,12},{5,13},{6,14},{7,15},{8,0},{9,1},... | collective-permute-start | bytes 1179656 | tf_op jit(solution)/shard_map/ppermute | solution.py:364
  51.8 5.5 %collective-permute-start.17 = (bf16[512,128]{1,0:T(8,128)(2,1)S(1)}, bf16[512,128]{1,0:T(8,128)(2,1)S(1)}, u32[]{:S(2)}, u32[]{:S(2)}) collective-permute-start(bf16[512,128]{1,0:T(8,128)(2,1)S(1)} %get-tuple-element.67), channel_id=1, source_target_pairs={{0,2},{1,3},{2,0},{3,1},{4,6},{5,7},{6,4},{7,5},{8,10},{9,11},{10,... | collective-permute-start | bytes 393224 | tf_op jit(solution)/shard_map/ppermute | solution.py:364
  53.1 11.2 %collective-permute-start.18 = (bf16[512,128]{1,0:T(8,128)(2,1)S(1)}, bf16[512,128]{1,0:T(8,128)(2,1)S(1)}, u32[]{:S(2)}, u32[]{:S(2)}) collective-permute-start(bf16[512,128]{1,0:T(8,128)(2,1)S(1)} %get-tuple-element.68), channel_id=1, source_target_pairs={{0,4},{1,5},{2,6},{3,7},{4,0},{5,1},{6,2},{7,3},{8,12},{9,13},{10,... | collective-permute-start | bytes 393224 | tf_op jit(solution)/shard_map/ppermute | solution.py:364
  55.9 10.7 %collective-permute-start.19 = (bf16[512,128]{1,0:T(8,128)(2,1)S(1)}, bf16[512,128]{1,0:T(8,128)(2,1)S(1)}, u32[]{:S(2)}, u32[]{:S(2)}) collective-permute-start(bf16[512,128]{1,0:T(8,128)(2,1)S(1)} %get-tuple-element.69), channel_id=1, source_target_pairs={{0,6},{1,7},{2,4},{3,5},{4,2},{5,3},{6,0},{7,1},{8,14},{9,15},{10,... | collective-permute-start | bytes 393224 | tf_op jit(solution)/shard_map/ppermute | solution.py:364
  66.6 9.1 %collective-permute-start.20 = (bf16[1024,128]{1,0:T(8,128)(2,1)S(1)}, bf16[1024,128]{1,0:T(8,128)(2,1)S(1)}, u32[]{:S(2)}, u32[]{:S(2)}) collective-permute-start(bf16[1024,128]{1,0:T(8,128)(2,1)S(1)} %for_mate.1), channel_id=1, source_target_pairs={{0,1},{1,0},{2,3},{3,2},{4,5},{5,4},{6,7},{7,6},{8,9},{9,8},{10,11... | collective-permute-start | bytes 786440 | tf_op jit(solution)/shard_map/ppermute | solution.py:364
  73.9 6.4 %collective-permute-start.23 = (bf16[512,128]{1,0:T(8,128)(2,1)S(1)}, bf16[512,128]{1,0:T(8,128)(2,1)S(1)}, u32[]{:S(2)}, u32[]{:S(2)}) collective-permute-start(bf16[512,128]{1,0:T(8,128)(2,1)S(1)} %get-tuple-element.78), channel_id=1, source_target_pairs={{0,2},{1,3},{2,0},{3,1},{4,6},{5,7},{6,4},{7,5},{8,10},{9,11},{10,... | collective-permute-start | bytes 393224 | tf_op jit(solution)/shard_map/ppermute | solution.py:364
  74.0 8.2 %collective-permute-start.24 = (bf16[512,128]{1,0:T(8,128)(2,1)S(1)}, bf16[512,128]{1,0:T(8,128)(2,1)S(1)}, u32[]{:S(2)}, u32[]{:S(2)}) collective-permute-start(bf16[512,128]{1,0:T(8,128)(2,1)S(1)} %get-tuple-element.79), channel_id=1, source_target_pairs={{0,3},{1,2},{2,1},{3,0},{4,7},{5,6},{6,5},{7,4},{8,11},{9,10},{10,... | collective-permute-start | bytes 393224 | tf_op jit(solution)/shard_map/ppermute | solution.py:364
  75.7 6.4 %collective-permute-start.25 = (bf16[512,128]{1,0:T(8,128)(2,1)S(1)}, bf16[512,128]{1,0:T(8,128)(2,1)S(1)}, u32[]{:S(2)}, u32[]{:S(2)}) collective-permute-start(bf16[512,128]{1,0:T(8,128)(2,1)S(1)} %get-tuple-element.80), channel_id=1, source_target_pairs={{0,4},{1,5},{2,6},{3,7},{4,0},{5,1},{6,2},{7,3},{8,12},{9,13},{10,... | collective-permute-start | bytes 393224 | tf_op jit(solution)/shard_map/ppermute | solution.py:364
  75.7 8.0 %collective-permute-start.26 = (bf16[512,128]{1,0:T(8,128)(2,1)S(1)}, bf16[512,128]{1,0:T(8,128)(2,1)S(1)}, u32[]{:S(2)}, u32[]{:S(2)}) collective-permute-start(bf16[512,128]{1,0:T(8,128)(2,1)S(1)} %get-tuple-element.81), channel_id=1, source_target_pairs={{0,5},{1,4},{2,7},{3,6},{4,1},{5,0},{6,3},{7,2},{8,13},{9,12},{10,... | collective-permute-start | bytes 393224 | tf_op jit(solution)/shard_map/ppermute | solution.py:364
  77.4 10.0 %collective-permute-start.27 = (bf16[512,128]{1,0:T(8,128)(2,1)S(1)}, bf16[512,128]{1,0:T(8,128)(2,1)S(1)}, u32[]{:S(2)}, u32[]{:S(2)}) collective-permute-start(bf16[512,128]{1,0:T(8,128)(2,1)S(1)} %get-tuple-element.82), channel_id=1, source_target_pairs={{0,6},{1,7},{2,4},{3,5},{4,2},{5,3},{6,0},{7,1},{8,14},{9,15},{10,... | collective-permute-start | bytes 393224 | tf_op jit(solution)/shard_map/ppermute | solution.py:364
  80.2 8.4 %collective-permute-start.28 = (bf16[512,128]{1,0:T(8,128)(2,1)S(1)}, bf16[512,128]{1,0:T(8,128)(2,1)S(1)}, u32[]{:S(2)}, u32[]{:S(2)}) collective-permute-start(bf16[512,128]{1,0:T(8,128)(2,1)S(1)} %get-tuple-element.83), channel_id=1, source_target_pairs={{0,7},{1,6},{2,5},{3,4},{4,3},{5,2},{6,1},{7,0},{8,15},{9,14},{10,... | collective-permute-start | bytes 393224 | tf_op jit(solution)/shard_map/ppermute | solution.py:364
  (9 other events, 43.9 us)
